TPU v7x, 256 devices: a whole 4x4x8 slice. The times are simulated.
256 devices in a mesh: blk: 64 (over z_hi, y, x), view: 4 (over z_lo, core).
Axes of the slice: x: 4, y: 4, z: 8 (z_hi: 4, z_lo: 2; z = z_hi * 2 + z_lo), core: 2. Of those that a mesh axis runs over, the one named last changes fastest.
Arguments:
- estimate: float32 [1024, 128, 128], P('blk'), may hold values from 0.2 to 5
- recorded: float32 [4, 1024, 128, 128], P('view', 'blk'), may hold values from 0.2 to 5
- offsets: int32 [4, 3], P('view'), may hold values from -16 to 16, as said below
- psf_z: float32 [4, 31], P('view'), may hold values from 0.05 to 1
- psf_y: float32 [4, 31], P('view'), may hold values from 0.05 to 1
- psf_x: float32 [4, 31], P('view'), may hold values from 0.05 to 1
- view_weights: float32 [4], P('view'), may hold values from 0.5 to 2
Outputs:
- deconvolved: float32 [1024, 128, 128], P('blk')
Inputs may be any that keep to these rules, and one draw needn't show every extreme that they name: offsets[v, 0] lies within -16 to 16, and in every draw one view has exactly 16 and another exactly -16; offsets[v, 1] and offsets[v, 2] lie within -8 to 8.
All inputs are finite; a program needn't handle non-finite values.
Results may differ from a plain program's by a relative error of at most 0.0001.
Values sent between devices are 32-bit elements; how exact they have to be, the bound alone decides.
No kernel may reach another device: no remote copies, remote signals or barrier semaphores. Data moves between devices by JAX's collectives and lax.ppermute only.
A program may use at most 64 MiB of HBM per device.

v0:
```python
import jax
import jax.numpy as jnp
from jax import lax
from jax.sharding import PartitionSpec as P

ITERS = 2


plane_pad = 8


def extended(x, sides, width):
    for axis, dim in sides:
        size, length = (lax.axis_size(axis), x.shape[dim])
        up = [(i, (i + 1) % size) for i in range(size - 1)]
        down = [(j, i) for i, j in up]
        last = lax.slice_in_dim(x, length - width, length, axis=dim)
        first = lax.slice_in_dim(x, 0, width, axis=dim)
        before = lax.ppermute(last, axis, up)
        after = lax.ppermute(first, axis, down)
        x = jnp.concatenate([before, x, after], axis=dim)
    return x


def band(taps, count):
    width = taps.shape[0]
    half = (width - 1) // 2
    rows = jnp.arange(count, dtype=jnp.int32)[:, None]
    cols = jnp.arange(count, dtype=jnp.int32)[None, :]
    place = cols - rows + half
    inside = (place >= 0) & (place < width)
    return jnp.where(inside, taps[jnp.clip(place, 0, width - 1)], jnp.zeros((), taps.dtype))


def slab_sum(padded, taps, count, adjoint):
    width = taps.shape[0]
    half = (width - 1) // 2
    total = jnp.zeros((count,) + padded.shape[1:], jnp.float32)
    for tap in range(width):
        start = 2 * half - tap if adjoint else tap
        total = total + taps[tap] * padded[start : start + count]
    return total


def plane_pass(field, mat_y, mat_x):
    inner = jnp.einsum("ij,zjx->zix", mat_y, field, precision=lax.Precision.HIGHEST)
    return jnp.einsum("zyj,ij->zyi", inner, mat_x, precision=lax.Precision.HIGHEST)


def blur_forward(field, taps_z, mat_y, mat_x):
    half = (taps_z.shape[0] - 1) // 2
    padded = extended(field, (("blk", 0),), half)
    summed = slab_sum(padded, taps_z, field.shape[0], False)
    return plane_pass(summed, mat_y, mat_x)


def blur_adjoint(field, taps_z, mat_y, mat_x):
    half = (taps_z.shape[0] - 1) // 2
    padded = extended(field, (("blk", 0),), half)
    summed = slab_sum(padded, taps_z, field.shape[0], True)
    return plane_pass(summed, mat_y.T, mat_x.T)


def cut_window(padded, count, shift, sign, shape):
    planes = jnp.pad(padded, ((0, 0), (plane_pad, plane_pad), (plane_pad, plane_pad)))
    starts = (count - sign * shift[0], plane_pad - sign * shift[1], plane_pad - sign * shift[2])
    starts = tuple((jnp.asarray(s) for s in starts))
    return lax.dynamic_slice(planes, starts, shape)


def per_device(estimate, recorded, offsets, psf_z, psf_y, psf_x, view_weights):
    taps_z = psf_z[0] / jnp.sum(psf_z[0])
    taps_y = psf_y[0] / jnp.sum(psf_y[0])
    taps_x = psf_x[0] / jnp.sum(psf_x[0])
    mat_y = band(taps_y, estimate.shape[1])
    mat_x = band(taps_x, estimate.shape[2])
    shift = offsets[0]
    weight = view_weights[0]
    wsum = lax.psum(view_weights[0], "view")
    image = recorded[0]
    count = estimate.shape[0]
    slab_total = count * lax.axis_size("blk")
    first_row = lax.axis_index("blk") * count
    zpos = first_row + jnp.arange(count, dtype=jnp.int32)[:, None, None] - shift[0]
    ypos = jnp.arange(estimate.shape[1], dtype=jnp.int32)[None, :, None] - shift[1]
    xpos = jnp.arange(estimate.shape[2], dtype=jnp.int32)[None, None, :] - shift[2]
    valid = (
        (zpos >= 0)
        & (zpos < slab_total)
        & (ypos >= 0)
        & (ypos < estimate.shape[1])
        & (xpos >= 0)
        & (xpos < estimate.shape[2])
    )
    for step in range(ITERS):
        blurred = blur_forward(estimate, taps_z, mat_y, mat_x)
        beside_all = extended(blurred, (("blk", 0),), count)
        forward = cut_window(beside_all, count, shift, 1, estimate.shape)
        safe = jnp.where(valid, forward, jnp.ones((), jnp.float32))
        ratio = jnp.where(valid, image / safe, jnp.zeros((), jnp.float32))
        returned = extended(ratio, (("blk", 0),), count)
        back = cut_window(returned, count, shift, -1, estimate.shape)
        back = blur_adjoint(back, taps_z, mat_y, mat_x)
        total = lax.psum(weight * back, "view")
        estimate = estimate * total / wsum
    return estimate


def solution(mesh):
    in_specs = (
        P("blk", None, None),
        P("view", "blk", None, None),
        P("view", None),
        P("view", None),
        P("view", None),
        P("view", None),
        P("view"),
    )
    out_specs = P("blk", None, None)
    return jax.shard_map(
        per_device, mesh=mesh, in_specs=in_specs, out_specs=out_specs, check_vma=False
    )
```

profile of v0, /device:TPU:95, one launch (start us, length us, event | category | flops | bytes accessed | tf_op | source)
XLA Modules:
  0.0 824.6 jit_solution(8588078122903690365)
XLA Ops:
  19.7 97.2 %gather_fusion.1 = f32[16384]{0:T(1024)S(1)} fusion(f32[31]{0:T(128)S(1)} %divide_bitcast_fusion, s32[16384]{0:T(1024)S(1)} %fusion.604), kind=kCustom, calls=%fused_computation.1 | custom fusion | bytes 196608 | tf_op jit(solution)/shard_map/gather | solution.py:32
  117.5 97.2 %gather_fusion = f32[16384]{0:T(1024)S(1)} fusion(f32[31]{0:T(128)S(1)} %divide_bitcast_fusion.1, s32[16384]{0:T(1024)S(1)} %fusion.604), kind=kCustom, calls=%fused_computation | custom fusion | bytes 196608 | tf_op jit(solution)/shard_map/gather | solution.py:32
  217.9 24.6 %convolution_bitcast_fusion.3 = f32[16,128,128]{2,1,0:T(8,128)S(1)} fusion(f32[31,128,128]{2,1,0:T(8,128)S(1)} %constant_dynamic-update-slice_fusion.2, f32[31,128,128]{2,1,0:T(8,128)S(1)} %get-tuple-element.11, f32[16,128,128]{2,1,0:T(8,128)S(1)} %copy-done, f32[]{:T(128)} %bitcast.35, f32[]{:T(128)} %bitcast.34, f32[]{:T(128)} %bitcast.33, f32[]{:T(128)} %bitcast.32, ...), kind=kOutput, calls=%fused_computation.189 | convolution fusion | flops 418742272 | bytes 33620092 | tf_op jit(solution)/shard_map/ij,zjx->zix/dot_general | solution.py:46
  246.5 9.7 %collective-permute-start.2 = (f32[16,128,128]{2,1,0:T(8,128)}, f32[16,128,128]{2,1,0:T(8,128)}, u32[]{:S(2)}, u32[]{:S(2)}) collective-permute-start(f32[16,128,128]{2,1,0:T(8,128)} %fusion.609), channel_id=1, source_target_pairs={{0,4},{4,8},{8,12},{12,16},{16,20},{20,24},{24,28},{28,32},{32,36}... | collective-permute-start | bytes 3145736 | tf_op jit(solution)/shard_map/ppermute | solution.py:19
  262.8 36.9 %collective-permute-done.3 = f32[16,128,128]{2,1,0:T(8,128)} collective-permute-done((f32[16,128,128]{2,1,0:T(8,128)}, f32[16,128,128]{2,1,0:T(8,128)}, u32[]{:S(2)}, u32[]{:S(2)}) %collective-permute-start.3) | collective-permute-done | bytes 1048608 | tf_op jit(solution)/shard_map/ppermute | solution.py:20
  307.5 10.4 %collective-permute-start.4 = (f32[16,128,128]{2,1,0:T(8,128)}, f32[16,128,128]{2,1,0:T(8,128)}, u32[]{:S(2)}, u32[]{:S(2)}) collective-permute-start(f32[16,128,128]{2,1,0:T(8,128)} %fusion.348), channel_id=1, source_target_pairs={{0,4},{4,8},{8,12},{12,16},{16,20},{20,24},{24,28},{28,32},{32,36}... | collective-permute-start | bytes 3145736 | tf_op jit(solution)/shard_map/ppermute | solution.py:19
  319.8 42.5 %collective-permute-done.5 = f32[16,128,128]{2,1,0:T(8,128)} collective-permute-done((f32[16,128,128]{2,1,0:T(8,128)}, f32[16,128,128]{2,1,0:T(8,128)}, u32[]{:S(2)}, u32[]{:S(2)}) %collective-permute-start.5) | collective-permute-done | bytes 1048608 | tf_op jit(solution)/shard_map/ppermute | solution.py:20
  369.1 9.9 %collective-permute-start.7 = (f32[15,128,128]{2,1,0:T(8,128)S(1)}, f32[15,128,128]{2,1,0:T(8,128)S(1)}, u32[]{:S(2)}, u32[]{:S(2)}) collective-permute-start(f32[15,128,128]{2,1,0:T(8,128)S(1)} %get-tuple-element.10), channel_id=1, source_target_pairs={{0,4},{4,8},{8,12},{12,16},{16,20},{20,24},{24,28},{28,32},{32,36}... | collective-permute-start | bytes 2949128 | tf_op jit(solution)/shard_map/ppermute | solution.py:19
  379.6 33.8 %collective-permute-done.6 = f32[15,128,128]{2,1,0:T(8,128)S(1)} collective-permute-done((f32[15,128,128]{2,1,0:T(8,128)S(1)}, f32[15,128,128]{2,1,0:T(8,128)S(1)}, u32[]{:S(2)}, u32[]{:S(2)}) %collective-permute-start.6) | collective-permute-done | bytes 983072 | tf_op jit(solution)/shard_map/ppermute | solution.py:20
  418.4 23.0 %convolution_bitcast_fusion.2 = f32[16,128,128]{2,1,0:T(8,128)S(1)} fusion(f32[16,128,128]{2,1,0:T(8,128)S(1)} %fusion.356, f32[15,128,128]{2,1,0:T(8,128)S(1)} %collective-permute-done.7, f32[15,128,128]{2,1,0:T(8,128)S(1)} %collective-permute-done.6, f32[]{:T(128)} %bitcast.35, f32[]{:T(128)} %bitcast.34, f32[]{:T(128)} %bitcast.33, f32[]{:T(128)} %bitcast.32, ...), kind=kOutput, calls=%fused_computation.188 | convolution fusion | flops 426606592 | bytes 4128892 | tf_op jit(solution)/shard_map/ij,zjx->zix/dot_general | solution.py:46
  443.4 9.0 %psum.22 = f32[]{:T(128)} all-reduce(f32[]{:T(128)} %bitcast), channel_id=1, replica_groups=mesh['blk'=64,'view'=4] {'view'}, use_global_device_ids=true, to_apply=%region_4.5 | all-reduce | flops 1 | bytes 8 | tf_op jit(solution)/shard_map/psum | solution.py:79
  452.5 41.6 %all-reduce.7.cloned.1.call-done = f32[16,128,128]{2,1,0:T(8,128)} async-done(((f32[16,128,128]{2,1,0:T(8,128)}), f32[16,128,128]{2,1,0:T(8,128)}) %all-reduce.7.cloned.1.call-update) | async-done | bytes 1048592 | tf_op jit(solution)/shard_map/psum | solution.py:104
  502.9 19.0 %collective-permute-done.8 = f32[15,128,128]{2,1,0:T(8,128)S(1)} collective-permute-done((f32[15,128,128]{2,1,0:T(8,128)S(1)}, f32[15,128,128]{2,1,0:T(8,128)S(1)}, u32[]{:S(2)}, u32[]{:S(2)}) %collective-permute-start.8) | collective-permute-done | bytes 983072 | tf_op jit(solution)/shard_map/ppermute | solution.py:19
  521.9 30.8 %collective-permute-done.9 = f32[15,128,128]{2,1,0:T(8,128)S(1)} collective-permute-done((f32[15,128,128]{2,1,0:T(8,128)S(1)}, f32[15,128,128]{2,1,0:T(8,128)S(1)}, u32[]{:S(2)}, u32[]{:S(2)}) %collective-permute-start.9) | collective-permute-done | bytes 983072 | tf_op jit(solution)/shard_map/ppermute | solution.py:20
  552.7 23.1 %convolution_bitcast_fusion.1 = f32[16,128,128]{2,1,0:T(8,128)S(1)} fusion(f32[16,128,128]{2,1,0:T(8,128)S(1)} %multiply_divide_fusion.1, f32[15,128,128]{2,1,0:T(8,128)S(1)} %collective-permute-done.9, f32[15,128,128]{2,1,0:T(8,128)S(1)} %collective-permute-done.8, f32[]{:T(128)} %bitcast.35, f32[]{:T(128)} %bitcast.34, f32[]{:T(128)} %bitcast.33, ...), kind=kOutput, calls=%fused_computation.186 | convolution fusion | flops 426606592 | bytes 4128892 | tf_op jit(solution)/shard_map/ij,zjx->zix/dot_general | solution.py:46
  578.7 9.9 %collective-permute-start.10 = (f32[16,128,128]{2,1,0:T(8,128)S(1)}, f32[16,128,128]{2,1,0:T(8,128)S(1)}, u32[]{:S(2)}, u32[]{:S(2)}) collective-permute-start(f32[16,128,128]{2,1,0:T(8,128)S(1)} %fusion.606), channel_id=1, source_target_pairs={{0,4},{4,8},{8,12},{12,16},{16,20},{20,24},{24,28},{28,32},{32,36}... | collective-permute-start | bytes 3145736 | tf_op jit(solution)/shard_map/ppermute | solution.py:19
  588.6 34.5 %collective-permute-done.11 = f32[16,128,128]{2,1,0:T(8,128)S(1)} collective-permute-done((f32[16,128,128]{2,1,0:T(8,128)S(1)}, f32[16,128,128]{2,1,0:T(8,128)S(1)}, u32[]{:S(2)}, u32[]{:S(2)}) %collective-permute-start.11) | collective-permute-done | bytes 1048608 | tf_op jit(solution)/shard_map/ppermute | solution.py:20
  629.5 10.6 %collective-permute-start.12 = (f32[16,128,128]{2,1,0:T(8,128)S(1)}, f32[16,128,128]{2,1,0:T(8,128)S(1)}, u32[]{:S(2)}, u32[]{:S(2)}) collective-permute-start(f32[16,128,128]{2,1,0:T(8,128)S(1)} %fusion.367), channel_id=1, source_target_pairs={{0,4},{4,8},{8,12},{12,16},{16,20},{20,24},{24,28},{28,32},{32,36}... | collective-permute-start | bytes 3145736 | tf_op jit(solution)/shard_map/ppermute | solution.py:19
  640.0 34.3 %collective-permute-done.13 = f32[16,128,128]{2,1,0:T(8,128)S(1)} collective-permute-done((f32[16,128,128]{2,1,0:T(8,128)S(1)}, f32[16,128,128]{2,1,0:T(8,128)S(1)}, u32[]{:S(2)}, u32[]{:S(2)}) %collective-permute-start.13) | collective-permute-done | bytes 1048608 | tf_op jit(solution)/shard_map/ppermute | solution.py:20
  688.8 10.6 %collective-permute-start.15 = (f32[15,128,128]{2,1,0:T(8,128)S(1)}, f32[15,128,128]{2,1,0:T(8,128)S(1)}, u32[]{:S(2)}, u32[]{:S(2)}) collective-permute-start(f32[15,128,128]{2,1,0:T(8,128)S(1)} %get-tuple-element.6), channel_id=1, source_target_pairs={{0,4},{4,8},{8,12},{12,16},{16,20},{20,24},{24,28},{28,32},{32,36}... | collective-permute-start | bytes 2949128 | tf_op jit(solution)/shard_map/ppermute | solution.py:19
  699.4 30.3 %collective-permute-done.14 = f32[15,128,128]{2,1,0:T(8,128)S(1)} collective-permute-done((f32[15,128,128]{2,1,0:T(8,128)S(1)}, f32[15,128,128]{2,1,0:T(8,128)S(1)}, u32[]{:S(2)}, u32[]{:S(2)}) %collective-permute-start.14) | collective-permute-done | bytes 983072 | tf_op jit(solution)/shard_map/ppermute | solution.py:20
  729.7 8.8 %collective-permute-done.15 = f32[15,128,128]{2,1,0:T(8,128)S(1)} collective-permute-done((f32[15,128,128]{2,1,0:T(8,128)S(1)}, f32[15,128,128]{2,1,0:T(8,128)S(1)}, u32[]{:S(2)}, u32[]{:S(2)}) %collective-permute-start.15) | collective-permute-done | bytes 983072 | tf_op jit(solution)/shard_map/ppermute | solution.py:19
  738.5 23.0 %convolution_bitcast_fusion = f32[16,128,128]{2,1,0:T(8,128)S(1)} fusion(f32[16,128,128]{2,1,0:T(8,128)S(1)} %fusion.375, f32[15,128,128]{2,1,0:T(8,128)S(1)} %collective-permute-done.15, f32[15,128,128]{2,1,0:T(8,128)S(1)} %collective-permute-done.14, f32[]{:T(128)} %bitcast.35, f32[]{:T(128)} %bitcast.34, f32[]{:T(128)} %bitcast.33, f32[]{:T(128)} %bitcast.32, ...), kind=kOutput, calls=%fused_computation.185 | convolution fusion | flops 426606592 | bytes 4128892 | tf_op jit(solution)/shard_map/ij,zjx->zix/dot_general | solution.py:46
  763.6 51.3 %all-reduce.9.cloned.1.call-done = f32[16,128,128]{2,1,0:T(8,128)} async-done(((f32[16,128,128]{2,1,0:T(8,128)}), f32[16,128,128]{2,1,0:T(8,128)}) %all-reduce.9.cloned.1.call-update) | async-done | bytes 1048592 | tf_op jit(solution)/shard_map/psum | solution.py:104
  (69 shorter events, 82.6 us)
Async XLA Ops:
  6.5 11.3 %copy-start.6 = (f32[1,31]{1,0:T(1,128)S(1)}, f32[1,31]{1,0:T(1,128)}, u32[]{:S(2)}) copy-start(f32[1,31]{1,0:T(1,128)} %param.11) | copy-start | bytes 376
  6.5 11.9 %copy-start.7 = (f32[1,31]{1,0:T(1,128)S(1)}, f32[1,31]{1,0:T(1,128)}, u32[]{:S(2)}) copy-start(f32[1,31]{1,0:T(1,128)} %param.10) | copy-start | bytes 376
  6.5 487.5 %all-reduce.7.cloned.1.call-start = ((), (), s32[]{:S(2)}) async-start(), calls=%async_computation | async-start | bytes 2097152 | tf_op jit(solution)/shard_map/psum | solution.py:104
  9.6 207.9 %collective-permute-start = (f32[15,128,128]{2,1,0:T(8,128)}, f32[15,128,128]{2,1,0:T(8,128)S(1)}, u32[]{:S(2)}, u32[]{:S(2)}) collective-permute-start(f32[15,128,128]{2,1,0:T(8,128)} %get-tuple-element.13), channel_id=1, source_target_pairs={{0,4},{4,8},{8,12},{12,16},{16,20},{20,24},{24,28},{28,32},{32,36}... | collective-permute-start | bytes 2949128 | tf_op jit(solution)/shard_map/ppermute | solution.py:19
  15.2 202.6 %collective-permute-start.1 = (f32[15,128,128]{2,1,0:T(8,128)}, f32[15,128,128]{2,1,0:T(8,128)S(1)}, u32[]{:S(2)}, u32[]{:S(2)}) collective-permute-start(f32[15,128,128]{2,1,0:T(8,128)} %get-tuple-element.14), channel_id=1, source_target_pairs={{4,0},{8,4},{12,8},{16,12},{20,16},{24,20},{28,24},{32,28},{36,32}... | collective-permute-start | bytes 2949128 | tf_op jit(solution)/shard_map/ppermute | solution.py:20
  117.5 97.2 %copy-start.4 = (s32[1,3]{1,0:T(1,128)S(1)}, s32[1,3]{1,0:T(1,128)}, u32[]{:S(2)}) copy-start(s32[1,3]{1,0:T(1,128)} %param.9) | copy-start | bytes 40
  244.6 55.1 %collective-permute-start.3 = (f32[16,128,128]{2,1,0:T(8,128)}, f32[16,128,128]{2,1,0:T(8,128)}, u32[]{:S(2)}, u32[]{:S(2)}) collective-permute-start(f32[16,128,128]{2,1,0:T(8,128)} %fusion.609), channel_id=1, source_target_pairs={{4,0},{8,4},{12,8},{16,12},{20,16},{24,20},{28,24},{32,28},{36,32}... | collective-permute-start | bytes 3145736 | tf_op jit(solution)/shard_map/ppermute | solution.py:20
  246.5 53.7 %collective-permute-start.2 = (f32[16,128,128]{2,1,0:T(8,128)}, f32[16,128,128]{2,1,0:T(8,128)}, u32[]{:S(2)}, u32[]{:S(2)}) collective-permute-start(f32[16,128,128]{2,1,0:T(8,128)} %fusion.609), channel_id=1, source_target_pairs={{0,4},{4,8},{8,12},{12,16},{16,20},{20,24},{24,28},{28,32},{32,36}... | collective-permute-start | bytes 3145736 | tf_op jit(solution)/shard_map/ppermute | solution.py:19
  262.8 42.8 %copy-start.2 = (pred[48,144,144]{2,1,0:T(8,128)(4,1)}, pred[48,144,144]{2,1,0:T(8,128)(4,1)S(1)}, u32[]{:S(2)}) copy-start(pred[48,144,144]{2,1,0:T(8,128)(4,1)S(1)} %get-tuple-element.54) | copy-start | bytes 2985988
  262.8 99.5 %copy-start.1 = (pred[48,144,144]{2,1,0:T(8,128)(4,1)}, pred[48,144,144]{2,1,0:T(8,128)(4,1)S(1)}, u32[]{:S(2)}) copy-start(pred[48,144,144]{2,1,0:T(8,128)(4,1)S(1)} %get-tuple-element.53) | copy-start | bytes 2985988
  305.6 56.7 %collective-permute-start.5 = (f32[16,128,128]{2,1,0:T(8,128)}, f32[16,128,128]{2,1,0:T(8,128)}, u32[]{:S(2)}, u32[]{:S(2)}) collective-permute-start(f32[16,128,128]{2,1,0:T(8,128)} %fusion.348), channel_id=1, source_target_pairs={{4,0},{8,4},{12,8},{16,12},{20,16},{24,20},{28,24},{32,28},{36,32}... | collective-permute-start | bytes 3145736 | tf_op jit(solution)/shard_map/ppermute | solution.py:20
  307.5 54.8 %collective-permute-start.4 = (f32[16,128,128]{2,1,0:T(8,128)}, f32[16,128,128]{2,1,0:T(8,128)}, u32[]{:S(2)}, u32[]{:S(2)}) collective-permute-start(f32[16,128,128]{2,1,0:T(8,128)} %fusion.348), channel_id=1, source_target_pairs={{0,4},{4,8},{8,12},{12,16},{16,20},{20,24},{24,28},{28,32},{32,36}... | collective-permute-start | bytes 3145736 | tf_op jit(solution)/shard_map/ppermute | solution.py:19
  367.1 46.2 %collective-permute-start.6 = (f32[15,128,128]{2,1,0:T(8,128)S(1)}, f32[15,128,128]{2,1,0:T(8,128)S(1)}, u32[]{:S(2)}, u32[]{:S(2)}) collective-permute-start(f32[15,128,128]{2,1,0:T(8,128)S(1)} %get-tuple-element.9), channel_id=1, source_target_pairs={{4,0},{8,4},{12,8},{16,12},{20,16},{24,20},{28,24},{32,28},{36,32}... | collective-permute-start | bytes 2949128 | tf_op jit(solution)/shard_map/ppermute | solution.py:20
  369.1 49.3 %collective-permute-start.7 = (f32[15,128,128]{2,1,0:T(8,128)S(1)}, f32[15,128,128]{2,1,0:T(8,128)S(1)}, u32[]{:S(2)}, u32[]{:S(2)}) collective-permute-start(f32[15,128,128]{2,1,0:T(8,128)S(1)} %get-tuple-element.10), channel_id=1, source_target_pairs={{0,4},{4,8},{8,12},{12,16},{16,20},{20,24},{24,28},{28,32},{32,36}... | collective-permute-start | bytes 2949128 | tf_op jit(solution)/shard_map/ppermute | solution.py:19
  443.4 371.4 %all-reduce.9.cloned.1.call-start = ((), (), s32[]{:S(2)}) async-start(), calls=%async_computation.1 | async-start | bytes 2097152 | tf_op jit(solution)/shard_map/psum | solution.py:104
  496.2 25.7 %collective-permute-start.8 = (f32[15,128,128]{2,1,0:T(8,128)S(1)}, f32[15,128,128]{2,1,0:T(8,128)S(1)}, u32[]{:S(2)}, u32[]{:S(2)}) collective-permute-start(f32[15,128,128]{2,1,0:T(8,128)S(1)} %get-tuple-element.7), channel_id=1, source_target_pairs={{0,4},{4,8},{8,12},{12,16},{16,20},{20,24},{24,28},{28,32},{32,36}... | collective-permute-start | bytes 2949128 | tf_op jit(solution)/shard_map/ppermute | solution.py:19
  501.0 51.7 %collective-permute-start.9 = (f32[15,128,128]{2,1,0:T(8,128)S(1)}, f32[15,128,128]{2,1,0:T(8,128)S(1)}, u32[]{:S(2)}, u32[]{:S(2)}) collective-permute-start(f32[15,128,128]{2,1,0:T(8,128)S(1)} %get-tuple-element.8), channel_id=1, source_target_pairs={{4,0},{8,4},{12,8},{16,12},{20,16},{24,20},{28,24},{32,28},{36,32}... | collective-permute-start | bytes 2949128 | tf_op jit(solution)/shard_map/ppermute | solution.py:20
  575.8 47.5 %copy-start.3 = (f32[1,16,128,128]{3,2,1,0:T(8,128)S(1)}, f32[1,16,128,128]{3,2,1,0:T(8,128)}, u32[]{:S(2)}) copy-start(f32[1,16,128,128]{3,2,1,0:T(8,128)} %param.8) | copy-start | bytes 3145732
  576.8 46.4 %collective-permute-start.11 = (f32[16,128,128]{2,1,0:T(8,128)S(1)}, f32[16,128,128]{2,1,0:T(8,128)S(1)}, u32[]{:S(2)}, u32[]{:S(2)}) collective-permute-start(f32[16,128,128]{2,1,0:T(8,128)S(1)} %fusion.606), channel_id=1, source_target_pairs={{4,0},{8,4},{12,8},{16,12},{20,16},{24,20},{28,24},{32,28},{36,32}... | collective-permute-start | bytes 3145736 | tf_op jit(solution)/shard_map/ppermute | solution.py:20
  578.7 44.6 %collective-permute-start.10 = (f32[16,128,128]{2,1,0:T(8,128)S(1)}, f32[16,128,128]{2,1,0:T(8,128)S(1)}, u32[]{:S(2)}, u32[]{:S(2)}) collective-permute-start(f32[16,128,128]{2,1,0:T(8,128)S(1)} %fusion.606), channel_id=1, source_target_pairs={{0,4},{4,8},{8,12},{12,16},{16,20},{20,24},{24,28},{28,32},{32,36}... | collective-permute-start | bytes 3145736 | tf_op jit(solution)/shard_map/ppermute | solution.py:19
  627.5 46.8 %collective-permute-start.13 = (f32[16,128,128]{2,1,0:T(8,128)S(1)}, f32[16,128,128]{2,1,0:T(8,128)S(1)}, u32[]{:S(2)}, u32[]{:S(2)}) collective-permute-start(f32[16,128,128]{2,1,0:T(8,128)S(1)} %fusion.367), channel_id=1, source_target_pairs={{4,0},{8,4},{12,8},{16,12},{20,16},{24,20},{28,24},{32,28},{36,32}... | collective-permute-start | bytes 3145736 | tf_op jit(solution)/shard_map/ppermute | solution.py:20
  629.5 53.0 %collective-permute-start.12 = (f32[16,128,128]{2,1,0:T(8,128)S(1)}, f32[16,128,128]{2,1,0:T(8,128)S(1)}, u32[]{:S(2)}, u32[]{:S(2)}) collective-permute-start(f32[16,128,128]{2,1,0:T(8,128)S(1)} %fusion.367), channel_id=1, source_target_pairs={{0,4},{4,8},{8,12},{12,16},{16,20},{20,24},{24,28},{28,32},{32,36}... | collective-permute-start | bytes 3145736 | tf_op jit(solution)/shard_map/ppermute | solution.py:19
  686.9 42.8 %collective-permute-start.14 = (f32[15,128,128]{2,1,0:T(8,128)S(1)}, f32[15,128,128]{2,1,0:T(8,128)S(1)}, u32[]{:S(2)}, u32[]{:S(2)}) collective-permute-start(f32[15,128,128]{2,1,0:T(8,128)S(1)} %get-tuple-element.5), channel_id=1, source_target_pairs={{4,0},{8,4},{12,8},{16,12},{20,16},{24,20},{28,24},{32,28},{36,32}... | collective-permute-start | bytes 2949128 | tf_op jit(solution)/shard_map/ppermute | solution.py:20
  688.8 49.7 %collective-permute-start.15 = (f32[15,128,128]{2,1,0:T(8,128)S(1)}, f32[15,128,128]{2,1,0:T(8,128)S(1)}, u32[]{:S(2)}, u32[]{:S(2)}) collective-permute-start(f32[15,128,128]{2,1,0:T(8,128)S(1)} %get-tuple-element.6), channel_id=1, source_target_pairs={{0,4},{4,8},{8,12},{12,16},{16,20},{20,24},{24,28},{28,32},{32,36}... | collective-permute-start | bytes 2949128 | tf_op jit(solution)/shard_map/ppermute | solution.py:19
  (2 other events, 13.5 us)
Sparse Core Ops, SparseCore 0:
  443.5 50.5 all-reduce.6
  763.7 51.0 all-reduce.8
where the time goes:
time: 828 us; the launch traced here: 825 us
  waiting for transfers between devices  377 us (46%)
  local copies, waits for them, and re-layouts  201 us (24%)
  matrix products  101 us (12%)
  starting transfers between devices  86.9 us (10%)
  other arithmetic  30 us (4%)
  between operations  20 us (2%)
  blocking collectives  9.04 us (1%)
    ppermute x8, waiting for transfers between devices, extended(): after = lax.ppermute(first, axis, down)  243 us
    gather x2, local copies, waits for them, and re-layouts, band(): taps[jnp.clip(place, 0, width - 1)]  194 us
    dot_general x4, matrix products, plane_pass(): jnp.einsum('ij,zjx->zix', mat_y, field, precision=lax.Precision.HIGHEST)  93.7 us
    psum x2, waiting for transfers between devices, per_device(): total = lax.psum(weight * back, 'view')  92.9 us
    ppermute x8, starting transfers between devices, extended(): before = lax.ppermute(last, axis, up)  71.5 us
    ppermute x8, waiting for transfers between devices, extended(): before = lax.ppermute(last, axis, up)  41.5 us
  transfers between devices with their start and end apart: 18, of which 15 were waited for; matrix products, arithmetic and copies ran while one was open for 25% of the time, Pallas kernels for 0%

commit v1 on v0

v1 whole, which is shorter than its diff:
```python
import jax
import jax.numpy as jnp
from jax import lax
from jax.experimental import pallas as pl
from jax.experimental.pallas import tpu as pltpu
from jax.sharding import PartitionSpec as P

ITERS = 2
TAPS = 31
HALF = 15
VIEWS = 4
BZ = 16
ROWS = 32
EXT = 64
LANES = 128
EDGE = 16
LAYERS = BZ + 2 * HALF
AXES = ("blk", "view")
HZ, HY, HX, WZ, MISC = 0, 1, 2, 3, 4
F32 = jnp.float32
BF16 = jnp.bfloat16

CELLS = [(z, y, x, v) for z in range(4) for y in range(4) for x in range(4) for v in range(4)]


def device(z, y, x, v):
    return ((z * 4 + y) * 4 + x) * 4 + v


PATH = ((0, 0), (1, 0), (1, 1), (2, 1), (2, 0), (3, 0), (3, 1), (0, 1))


def place(block, r):
    z, chip, core = block // 16, (block // 2) % 8, block % 2
    y, z_lo = PATH[chip]
    return device(z, y, r, 2 * z_lo + (core ^ (chip % 2)))


def spread(x, j):
    perm = [(device(z, y, c, v), place(16 * z + 4 * y + c, (v + j) % 4)) for z, y, c, v in CELLS]
    return lax.ppermute(x, AXES, perm)


def collect(x, j):
    perm = [(place(16 * z + 4 * y + q, r), device(z, y, q, (r + j) % 4)) for z, y, r, q in CELLS]
    return lax.ppermute(x, AXES, perm)


def view_swap(x, mask):
    return lax.ppermute(x, AXES, [(device(z, y, c, v), device(z, y, c, v ^ mask)) for z, y, c, v in CELLS])


def to_layer(x, step):
    perm = [(place(b, r), place((b + step) % 64, r)) for b in range(64) for r in range(4)]
    return lax.ppermute(x, AXES, perm)


def to_row(x, step):
    perm = [(place(b, r), place(b, (r + step) % 4)) for b in range(64) for r in range(4)]
    return lax.ppermute(x, AXES, perm)


def position():
    blk, view = lax.axis_index("blk"), lax.axis_index("view")
    y = lax.rem(lax.div(blk, 4), 4)
    near = jnp.where(y < 2, y, y + 2)
    far = jnp.where(y == 0, 7, jnp.where(y == 3, 6, y + 1))
    chip = jnp.where(view < 2, near, far)
    core = (view & 1) ^ (chip & 1)
    return view, lax.rem(blk, 4), lax.div(blk, 16) * 16 + 2 * chip + core


def vmem():
    return pl.BlockSpec(memory_space=pltpu.VMEM)


def smem():
    return pl.BlockSpec(memory_space=pltpu.SMEM)


def hbm():
    return pl.BlockSpec(memory_space=pl.ANY)


def call(body, outs, args, specs, scratch, flops, out_specs=None):
    size = sum(a.size * a.dtype.itemsize for a in args)
    return pl.pallas_call(
        body,
        out_shape=outs,
        in_specs=specs,
        out_specs=out_specs or jax.tree.map(lambda _: vmem(), outs),
        scratch_shapes=scratch,
        compiler_params=pltpu.CompilerParams(vmem_limit_bytes=48 * 1024 * 1024),
        cost_estimate=pl.CostEstimate(flops=flops, bytes_accessed=size, transcendentals=0),
    )(*args)


def shape(*dims, dtype=F32):
    return jax.ShapeDtypeStruct(dims, dtype)


def iota(dims, axis):
    return lax.broadcasted_iota(jnp.int32, dims, axis)


def pieces(x):
    high = x.astype(BF16)
    low = (x - high.astype(F32)).astype(BF16)
    return high, low


def prologue_body(offsets, weight, est, rec, psf_z, psf_y, psf_x, ext, o0, o1, o2, o3, held, moved, sems, sem):
    view = lax.axis_index("view")
    step = BZ // 4
    parts = [
        pltpu.make_async_copy(rec.at[0, pl.ds(k * step, step)], held.at[pl.ds(k * step, step)], sems.at[k])
        for k in range(4)
    ]
    for part in parts:
        part.start()

    def window(k):
        first = max(0, k * ROWS - EDGE)
        size = min(LANES, (k + 1) * ROWS + EDGE) - first
        skip = first - (k * ROWS - EDGE)
        return pltpu.make_async_copy(est.at[:, pl.ds(first, size)], ext.at[:, pl.ds(skip, size)], sem)

    for k in range(VIEWS):

        @pl.when(view == k)
        def _(k=k):
            window(k).start()
            if k == 0:
                ext[:, :EDGE, :] = jnp.zeros((BZ, EDGE, LANES), F32)
            if k == VIEWS - 1:
                ext[:, EXT - EDGE :, :] = jnp.zeros((BZ, EDGE, LANES), F32)

    dy, dx = offsets[0, 1], offsets[0, 2]
    row = iota((LANES, LANES), 0) + dy
    col = iota((LANES, LANES), 1) + dx
    inside = (row >= 0) & (row < LANES) & (col >= 0) & (col < LANES)
    back_y = lax.rem(LANES - dy, LANES)
    back_x = lax.rem(LANES - dx, LANES)

    for k, part in enumerate(parts):
        part.wait()

        @pl.loop(k * step, (k + 1) * step)
        def _(z):
            plane = pltpu.roll(pltpu.roll(held[z], back_y, 0), back_x, 1)
            moved[z] = jnp.where(inside, plane, 0.0)

    hz, hy, hx = (t[...] / jnp.sum(t[...], axis=1, keepdims=True) for t in (psf_z, psf_y, psf_x))
    lane = iota((1, LANES), 1)
    misc = jnp.where(lane == 0, weight[0], jnp.where(lane == 1, offsets[0, 0].astype(F32), 0.0))
    for j, out in enumerate((o0, o1, o2, o3)):
        start = pl.multiple_of(lax.rem(view + j, VIEWS) * ROWS, ROWS)
        out[:BZ] = moved[:, pl.ds(start, ROWS), :]
        out[BZ] = jnp.zeros((ROWS, LANES), F32)
        out[BZ, HZ : HZ + 1, :TAPS] = hz
        out[BZ, HY : HY + 1, :TAPS] = hy
        out[BZ, HX : HX + 1, :TAPS] = hx
        out[BZ, WZ : WZ + 1, :TAPS] = weight[0] * hz
        out[BZ, MISC : MISC + 1, :] = misc

    for k in range(VIEWS):

        @pl.when(view == k)
        def _(k=k):
            window(k).wait()


def shift_of(taps, v):
    return taps[v, MISC, 1].astype(jnp.int32)


def pack_body(a0, a1, a2, a3, up, down, rec, taps, held, sems, tap_sems):
    blocks = (a0, a1, a2, a3)
    data = [pltpu.make_async_copy(a.at[pl.ds(0, BZ)], held.at[v], sems.at[v]) for v, a in enumerate(blocks)]
    rows = [
        pltpu.make_async_copy(a.at[BZ, pl.ds(0, 8)], taps.at[v], tap_sems.at[v]) for v, a in enumerate(blocks)
    ]
    for copy in rows + data:
        copy.start()
    for out in (up, down):
        out[BZ:] = jnp.zeros((2 * BZ, ROWS, LANES), F32)
    n_up, n_down = jnp.int32(0), jnp.int32(0)
    for v in range(VIEWS):
        rows[v].wait()
        data[v].wait()
        dz = shift_of(taps, v)

        @pl.when(dz < 0)
        def _(v=v, n=n_up):
            up[pl.ds(n * BZ, BZ)] = held[v]

        @pl.when(dz > 0)
        def _(v=v, n=n_down):
            down[pl.ds(n * BZ, BZ)] = held[v]

        n_up = n_up + jnp.where(dz < 0, 1, 0)
        n_down = n_down + jnp.where(dz > 0, 1, 0)

        @pl.loop(0, BZ)
        def _(i, v=v, dz=dz):
            src = i + dz
            rec[v, i] = jnp.where((src >= 0) & (src < BZ), held[v, jnp.clip(src, 0, BZ - 1)], 0.0)


def bands_body(taps, wy_f, wy_b, wx_f, wx_b):
    dims = (ROWS, 4 * EXT)
    lane = iota(dims, 1)
    gap = (lane & (EXT - 1)) - iota(dims, 0) - 1
    for v in range(VIEWS):
        band = jnp.zeros(dims, F32)
        for a in range(TAPS):
            band = jnp.where(gap == a, taps[v, HY, a], band)
        high = band.astype(BF16).astype(F32)
        wy_f[v * ROWS : (v + 1) * ROWS, :] = jnp.where(lane < 2 * EXT, high, band - high).astype(BF16)

    dims = (EXT, LANES)
    lane = iota(dims, 1)
    gap = iota(dims, 0) - (lane & (ROWS - 1)) - 1
    band = jnp.zeros(dims, F32)
    for a in range(TAPS):
        tap = jnp.zeros((1, LANES), F32)
        for v in range(VIEWS):
            tap = jnp.where(iota((1, LANES), 1) >= v * ROWS, taps[v, HY, a], tap)
        band = jnp.where(gap == a, tap, band)
    high, low = pieces(band)
    wy_b[...] = jnp.concatenate([jnp.concatenate([high, high], 1), jnp.concatenate([low, low], 1)], 0)

    dims = (LANES, LANES)
    gap = iota(dims, 0) - iota(dims, 1)
    for v in range(VIEWS):
        for out, sign in ((wx_f, 1), (wx_b, -1)):
            band = jnp.zeros(dims, F32)
            for a in range(TAPS):
                band = jnp.where(gap == sign * (a - HALF), taps[v, HX, a], band)
            high, low = pieces(band)
            part = jnp.concatenate([high, low], 1)
            out[v] = jnp.concatenate([part, part], 0)


def forward_body(taps, before, own, after, wy_f, wx_f, out, inner, summed):
    _, _, block = position()

    def layer(k):
        if k < HALF:
            return jnp.where(block > 0, before[k + 1], 0.0)
        if k < HALF + BZ:
            return own[k - HALF]
        return jnp.where(block < 63, after[k - HALF - BZ], 0.0)

    for p in range(LAYERS // 2):
        high, low = pieces(jnp.concatenate([layer(2 * p), layer(2 * p + 1)], 1))
        data = jnp.concatenate([high, low, high, low], 0)
        done = jnp.dot(wy_f[...], data, preferred_element_type=F32)
        for v in range(VIEWS):
            rows = done[v * ROWS : (v + 1) * ROWS]
            inner[v, 2 * p] = rows[:, :LANES]
            inner[v, 2 * p + 1] = rows[:, LANES:]

    @pl.loop(0, VIEWS * 4)
    def _(n):
        v = lax.div(n, 4)
        rows = pl.ds(pl.multiple_of(lax.rem(n, 4) * 8, 8), 8)
        hz = [taps[v, HZ, a] for a in range(TAPS)]
        acc = [None] * BZ
        for k in range(LAYERS):
            x = inner[v, k, rows, :]
            for i in range(max(0, k - TAPS + 1), min(BZ - 1, k) + 1):
                term = hz[k - i] * x
                acc[i] = term if acc[i] is None else acc[i] + term
        for i in range(BZ):
            summed[v, i, rows, :] = acc[i]

    for v in range(VIEWS):
        high, low = pieces(summed[v].reshape(BZ * ROWS, LANES))
        done = jnp.dot(jnp.concatenate([high, low], 1), wx_f[v], preferred_element_type=F32)
        out[v] = (done[:, :LANES] + done[:, LANES:]).reshape(BZ, ROWS, LANES)


def back_body(taps, fwd, rec, wx_b, wy_b, before, own, after, inner, spread_z):
    for v in range(VIEWS):
        ratio = (rec[v] / fwd[v]).reshape(BZ * ROWS, LANES)
        high, low = pieces(ratio)
        done = jnp.dot(jnp.concatenate([high, low], 1), wx_b[v], preferred_element_type=F32)
        inner[v] = (done[:, :LANES] + done[:, LANES:]).reshape(BZ, ROWS, LANES)

    @pl.loop(0, VIEWS * 4)
    def _(n):
        v = lax.div(n, 4)
        rows = pl.ds(pl.multiple_of(lax.rem(n, 4) * 8, 8), 8)
        place_rows = pl.ds(pl.multiple_of(n * 8, 8), 8)
        hz = [taps[v, WZ, a] for a in range(TAPS)]
        x = [inner[v, i, rows, :] for i in range(BZ)]
        for k in range(LAYERS):
            acc = None
            for i in range(max(0, k - TAPS + 1), min(BZ - 1, k) + 1):
                term = hz[k - i] * x[i]
                acc = term if acc is None else acc + term
            spread_z[k, place_rows, :] = acc

    def store(k, value):
        if k < HALF:
            before[k] = value
        elif k < HALF + BZ:
            own[k - HALF] = value
        else:
            after[k - HALF - BZ] = value

    for p in range(LAYERS // 2):
        high, low = pieces(jnp.concatenate([spread_z[2 * p], spread_z[2 * p + 1]], 1))
        done = jnp.dot(wy_b[...], jnp.concatenate([high, low], 0), preferred_element_type=F32)
        both = done[:EXT] + done[EXT:]
        store(2 * p, both[:, :LANES])
        store(2 * p + 1, both[:, LANES:])


def first_back_body(taps, fwd, part, lower, upper, wx_b, wy_b, *rest):
    before, own, after, rec, low, high, sems, inner, spread_z = rest
    _, _, block = position()
    copies = [pltpu.make_async_copy(lower, low, sems.at[0]), pltpu.make_async_copy(upper, high, sems.at[1])]
    for copy in copies:
        copy.start()
    for copy in copies:
        copy.wait()
    n_up, n_down = jnp.int32(0), jnp.int32(0)
    for v in range(VIEWS):
        dz = shift_of(taps, v)

        @pl.loop(0, BZ)
        def _(i, v=v, dz=dz, n_up=n_up, n_down=n_down):
            src = i + dz
            place_z = block * BZ + src
            x = part[v, i]
            x = jnp.where(src < 0, low[jnp.clip(n_up * BZ + src + BZ, 0, 3 * BZ - 1)], x)
            x = jnp.where(src >= BZ, high[jnp.clip(n_down * BZ + src - BZ, 0, 3 * BZ - 1)], x)
            rec[v, i] = jnp.where((place_z >= 0) & (place_z < 64 * BZ), x, 0.0)

        n_up = n_up + jnp.where(dz < 0, 1, 0)
        n_down = n_down + jnp.where(dz > 0, 1, 0)

    back_body(taps, fwd, rec, wx_b, wy_b, before, own, after, inner, spread_z)


def add_layers(own, from_prev, from_next, cut):
    _, _, block = position()
    out = []
    for i in range(BZ):
        value = own[i, cut]
        if i < HALF:
            value = value + jnp.where(block > 0, from_prev[i, cut], 0.0)
        if i > 0:
            value = value + jnp.where(block < 63, from_next[i - 1, cut], 0.0)
        out.append(value)
    return out


def halves_body(own, from_prev, from_next, low, high):
    for out, cut in ((low, slice(0, ROWS)), (high, slice(ROWS, EXT))):
        for i, value in enumerate(add_layers(own, from_prev, from_next, cut)):
            out[i] = value


def edges_body(own, from_prev, from_next, low, middle, high):
    cuts = (slice(0, EDGE), slice(EDGE, EXT - EDGE), slice(EXT - EDGE, EXT))
    for out, cut in zip((low, middle, high), cuts):
        for i, value in enumerate(add_layers(own, from_prev, from_next, cut)):
            out[i] = value


def view_sum(taps):
    return taps[0, MISC, 0] + taps[1, MISC, 0] + taps[2, MISC, 0] + taps[3, MISC, 0]


def window_body(taps, ext, low, high, from_prev, from_next, out):
    _, r, _ = position()
    wsum = view_sum(taps)
    for i in range(BZ):
        total = low[i] + jnp.where(r > 0, from_prev[i], 0.0)
        out[i, :ROWS] = ext[i, :ROWS] * total / wsum
        total = high[i] + jnp.where(r < 3, from_next[i], 0.0)
        out[i, ROWS:] = ext[i, ROWS:] * total / wsum


def last_body(taps, ext, middle, from_prev, from_next, out):
    _, r, _ = position()
    wsum = view_sum(taps)
    for i in range(BZ):
        total = middle[i, :EDGE] + jnp.where(r > 0, from_prev[i], 0.0)
        out[i, :EDGE] = ext[i, EDGE:ROWS] * total / wsum
        total = middle[i, EDGE:] + jnp.where(r < 3, from_next[i], 0.0)
        out[i, EDGE:] = ext[i, ROWS : EXT - EDGE] * total / wsum


def join_body(c0, c1, c2, c3, out):
    view = lax.axis_index("view")
    for mask, chunk in enumerate((c0, c1, c2, c3)):
        start = pl.multiple_of((view ^ mask) * ROWS, ROWS)
        out[:, pl.ds(start, ROWS), :] = chunk[...]


BLOCK = (VIEWS, BZ, ROWS, LANES)
INNER = (VIEWS, LAYERS, ROWS, LANES)
SPREAD = (LAYERS, LANES, LANES)
WINDOW = (BZ, EXT, LANES)
HALO = (HALF, EXT, LANES)
QUARTER = (BZ, ROWS, LANES)
PACKED = (3 * BZ, ROWS, LANES)
STRIP = (BZ, EDGE, LANES)


def per_device(estimate, recorded, offsets, psf_z, psf_y, psf_x, view_weights):
    with jax.named_scope("prologue"):
        ext, *chunks = call(
            prologue_body,
            (shape(*WINDOW),) + (shape(BZ + 1, ROWS, LANES),) * 4,
            (offsets, view_weights, estimate, recorded, psf_z, psf_y, psf_x),
            [smem(), smem(), hbm(), hbm()] + [vmem()] * 3,
            [
                pltpu.VMEM((BZ, LANES, LANES), F32),
                pltpu.VMEM((BZ, LANES, LANES), F32),
                pltpu.SemaphoreType.DMA((4,)),
                pltpu.SemaphoreType.DMA,
            ],
            10_000_000,
        )
    with jax.named_scope("spread"):
        ext = spread(ext, 0)
        mine = [spread(c, j) for j, c in enumerate(chunks)]
    with jax.named_scope("shift"):
        up, down, part, taps = call(
            pack_body,
            (shape(*PACKED), shape(*PACKED), shape(*BLOCK), shape(VIEWS, 8, LANES)),
            tuple(mine),
            [hbm()] * 4,
            [pltpu.VMEM(BLOCK, F32), pltpu.SemaphoreType.DMA((4,)), pltpu.SemaphoreType.DMA((4,))],
            10_000_000,
            (vmem(), vmem(), vmem(), smem()),
        )
        lower = to_layer(up, 1)
        upper = to_layer(down, -1)

    with jax.named_scope("bands"):
        wy_f, wy_b, wx_f, wx_b = call(
            bands_body,
            (
                shape(LANES, 4 * EXT, dtype=BF16),
                shape(LANES, 2 * LANES, dtype=BF16),
                shape(VIEWS, 2 * LANES, 2 * LANES, dtype=BF16),
                shape(VIEWS, 2 * LANES, 2 * LANES, dtype=BF16),
            ),
            (taps,),
            [smem()],
            [],
            30_000_000,
        )

    rec = None
    for step in range(ITERS):
        with jax.named_scope("layers_in"):
            before = to_layer(ext, 1)
            after = to_layer(ext, -1)
        with jax.named_scope("forward"):
            fwd = call(
                forward_body,
                shape(*BLOCK),
                (taps, before, ext, after, wy_f, wx_f),
                [smem()] + [vmem()] * 5,
                [pltpu.VMEM(INNER, F32), pltpu.VMEM(BLOCK, F32)],
                2_000_000_000,
            )
        with jax.named_scope("back"):
            outs = (shape(*HALO), shape(*WINDOW), shape(*HALO))
            scratch = [pltpu.VMEM(BLOCK, F32), pltpu.VMEM(SPREAD, F32)]
            if rec is None:
                c_before, c_own, c_after, rec = call(
                    first_back_body,
                    outs + (shape(*BLOCK),),
                    (taps, fwd, part, lower, upper, wx_b, wy_b),
                    [smem(), vmem(), vmem(), hbm(), hbm(), vmem(), vmem()],
                    [pltpu.VMEM(PACKED, F32), pltpu.VMEM(PACKED, F32), pltpu.SemaphoreType.DMA((2,))] + scratch,
                    2_000_000_000,
                )
            else:
                c_before, c_own, c_after = call(
                    back_body,
                    outs,
                    (taps, fwd, rec, wx_b, wy_b),
                    [smem()] + [vmem()] * 4,
                    scratch,
                    2_000_000_000,
                )
        with jax.named_scope("layers_out"):
            from_next = to_layer(c_before, -1)
            from_prev = to_layer(c_after, 1)
        if step < ITERS - 1:
            with jax.named_scope("rows"):
                low, high = call(
                    halves_body, (shape(*QUARTER),) * 2, (c_own, from_prev, from_next), [vmem()] * 3, [], 1_000_000
                )
                row_prev = to_row(high, 1)
                row_next = to_row(low, -1)
                ext = call(
                    window_body,
                    shape(*WINDOW),
                    (taps, ext, low, high, row_prev, row_next),
                    [smem()] + [vmem()] * 5,
                    [],
                    1_000_000,
                )
        else:
            with jax.named_scope("rows"):
                low, middle, high = call(
                    edges_body,
                    (shape(*STRIP), shape(*QUARTER), shape(*STRIP)),
                    (c_own, from_prev, from_next),
                    [vmem()] * 3,
                    [],
                    1_000_000,
                )
                row_prev = to_row(high, 1)
                row_next = to_row(low, -1)
                own = call(
                    last_body,
                    shape(*QUARTER),
                    (taps, ext, middle, row_prev, row_next),
                    [smem()] + [vmem()] * 4,
                    [],
                    1_000_000,
                )

    with jax.named_scope("result"):
        c0 = collect(own, 0)
        c1 = view_swap(c0, 1)
        c2 = view_swap(c0, 2)
        c3 = view_swap(c2, 1)
        return call(join_body, shape(BZ, LANES, LANES), (c0, c1, c2, c3), [vmem()] * 4, [], 1_000_000)


def solution(mesh):
    in_specs = (
        P("blk", None, None),
        P("view", "blk", None, None),
        P("view", None),
        P("view", None),
        P("view", None),
        P("view", None),
        P("view"),
    )
    out_specs = P("blk", None, None)
    return jax.shard_map(
        per_device, mesh=mesh, in_specs=in_specs, out_specs=out_specs, check_vma=False
    )
```

time: 828 us -> 170 us (0.21)
  the two profiles are of different devices: /device:TPU:95 before, /device:TPU:1 now
where the time goes in v1:
time: 170 us
  waiting for transfers between devices  70.9 us (42%)
  starting transfers between devices  65.4 us (38%)
  Pallas kernels  28.4 us (17%)
  local copies, waits for them, and re-layouts  4.07 us (2%)
    pallas_call x12, Pallas kernels, call(): pl.pallas_call(body, out_shape=outs, in_specs=specs, out_specs=out_specs...  28.4 us
    ppermute x5, waiting for transfers between devices, spread(): return lax.ppermute(x, AXES, perm)  26.9 us
    ppermute x10, starting transfers between devices, to_layer(): return lax.ppermute(x, AXES, perm)  25 us
    ppermute x10, waiting for transfers between devices, to_layer(): return lax.ppermute(x, AXES, perm)  23.5 us
    ppermute x5, starting transfers between devices, spread(): return lax.ppermute(x, AXES, perm)  16.5 us
    ppermute x1, starting transfers between devices, collect(): return lax.ppermute(x, AXES, perm)  13 us
    ppermute x4, waiting for transfers between devices, to_row(): return lax.ppermute(x, AXES, perm)  9.46 us
    ppermute x3, waiting for transfers between devices, view_swap(): lax.ppermute(x, AXES, [(device(z, y, c, v), device(z, y, c, v ^ mask)) fo...  6.9 us
  transfers between devices with their start and end apart: 23, of which 17 were waited for; matrix products, arithmetic and copies ran while one was open for 0% of the time, Pallas kernels for 5%

profile of v1, /device:TPU:1, one launch (start us, length us, event | category | flops | bytes accessed | tf_op | source)
XLA Modules:
  0.0 169.6 jit_solution(969376730482882359)
XLA Ops:
  6.2 4.5 %collective-permute-start.4 = (f32[16,64,128]{2,1,0:T(8,128)S(1)}, f32[16,64,128]{2,1,0:T(8,128)S(1)}, u32[]{:S(2)}, u32[]{:S(2)}) collective-permute-start(f32[16,64,128]{2,1,0:T(8,128)S(1)} %get-tuple-element.35), channel_id=1, source_target_pairs={{0,0},{1,4},{2,8},{3,12},{4,1},{5,5},{6,9},{7,13},{8,17},{9,21},{1... | collective-permute-start | bytes 1572872 | tf_op jit(solution)/shard_map/spread/ppermute | solution.py:41
  12.6 5.7 %collective-permute-start.1 = (f32[17,32,128]{2,1,0:T(8,128)S(1)}, f32[17,32,128]{2,1,0:T(8,128)S(1)}, u32[]{:S(2)}, u32[]{:S(2)}) collective-permute-start(f32[17,32,128]{2,1,0:T(8,128)S(1)} %get-tuple-element.31), channel_id=1, source_target_pairs={{0,4},{1,8},{2,12},{3,0},{4,5},{5,9},{6,13},{7,1},{8,21},{9,25},{1... | collective-permute-start | bytes 835592 | tf_op jit(solution)/shard_map/spread/ppermute | solution.py:41
  18.3 4.3 %collective-permute-start.2 = (f32[17,32,128]{2,1,0:T(8,128)S(1)}, f32[17,32,128]{2,1,0:T(8,128)S(1)}, u32[]{:S(2)}, u32[]{:S(2)}) collective-permute-start(f32[17,32,128]{2,1,0:T(8,128)S(1)} %get-tuple-element.32), channel_id=1, source_target_pairs={{0,8},{1,12},{2,0},{3,4},{4,9},{5,13},{6,1},{7,5},{8,25},{9,29},{1... | collective-permute-start | bytes 835592 | tf_op jit(solution)/shard_map/spread/ppermute | solution.py:41
  22.8 19.4 %collective-permute-done.a0 = f32[17,32,128]{2,1,0:T(8,128)S(1)} collective-permute-done((f32[17,32,128]{2,1,0:T(8,128)S(1)}, f32[17,32,128]{2,1,0:T(8,128)S(1)}, u32[]{:S(2)}, u32[]{:S(2)}) %collective-permute-start) | collective-permute-done | bytes 278560 | tf_op jit(solution)/shard_map/spread/ppermute | solution.py:41
  42.1 6.0 %collective-permute-done.2.a2 = f32[17,32,128]{2,1,0:T(8,128)S(1)} collective-permute-done((f32[17,32,128]{2,1,0:T(8,128)S(1)}, f32[17,32,128]{2,1,0:T(8,128)S(1)}, u32[]{:S(2)}, u32[]{:S(2)}) %collective-permute-start.2) | collective-permute-done | bytes 278560 | tf_op jit(solution)/shard_map/spread/ppermute | solution.py:41
  52.8 4.7 %collective-permute-start.7 = (f32[48,32,128]{2,1,0:T(8,128)S(1)}, f32[48,32,128]{2,1,0:T(8,128)S(1)}, u32[]{:S(2)}, u32[]{:S(2)}) collective-permute-start(f32[48,32,128]{2,1,0:T(8,128)S(1)} %get-tuple-element.39), channel_id=1, source_target_pairs={{0,1},{4,5},{8,9},{12,13},{1,17},{5,21},{9,25},{13,29},{17,16},{21... | collective-permute-start | bytes 2359304 | tf_op jit(solution)/shard_map/shift/ppermute | solution.py:55
  57.5 4.0 %collective-permute-start.6 = (f32[16,64,128]{2,1,0:T(8,128)S(1)}, f32[16,64,128]{2,1,0:T(8,128)S(1)}, u32[]{:S(2)}, u32[]{:S(2)}) collective-permute-start(f32[16,64,128]{2,1,0:T(8,128)S(1)} %collective-permute-done.4.own.ext), channel_id=1, source_target_pairs={{0,194},{4,198},{8,202},{12,206},{1,0},{5,4},{9,8},{13,12},{17,1},... | collective-permute-start | bytes 1572872 | tf_op jit(solution)/shard_map/layers_in/ppermute | solution.py:55
  63.8 10.5 %collective-permute-done.6.after = f32[16,64,128]{2,1,0:T(8,128)S(1)} collective-permute-done((f32[16,64,128]{2,1,0:T(8,128)S(1)}, f32[16,64,128]{2,1,0:T(8,128)S(1)}, u32[]{:S(2)}, u32[]{:S(2)}) %collective-permute-start.6) | collective-permute-done | bytes 524320 | tf_op jit(solution)/shard_map/layers_in/ppermute | solution.py:55
  74.3 4.5 %forward.2.fwd = f32[4,16,32,128]{3,2,1,0:T(8,128)S(1)} custom-call(f32[4,8,128]{2,1,0:T(8,128)S(1)} %get-tuple-element.34.taps, f32[16,64,128]{2,1,0:T(8,128)S(1)} %collective-permute-done.5.before, f32[16,64,128]{2,1,0:T(8,128)S(1)} %collective-permute-done.4.own.ext, f32[16,64,128]{2,1,0:T(8,128)S(1)} %collective-permute-done.6.after, ...), custom_call_target="tpu_custom_call" | custom-call | flops 2000000000 | bytes 2179072 | tf_op jit(solution)/shard_map/forward/pallas_call | solution.py:87
  78.8 5.5 %back.2 = (f32[15,64,128]{2,1,0:T(8,128)S(1)}, f32[16,64,128]{2,1,0:T(8,128)S(1)}, f32[15,64,128]{2,1,0:T(8,128)S(1)}, f32[4,16,32,128]{3,2,1,0:T(8,128)S(1)}) custom-call(f32[4,8,128]{2,1,0:T(8,128)S(1)} %get-tuple-element.34.taps, f32[4,16,32,128]{3,2,1,0:T(8,128)S(1)} %forward.2.fwd, f32[4,16,32,128]{3,2,1,0:T(8,128)} %copy-done.6, ...), custom_call_target="tpu_custom_call" | custom-call | flops 2000000000 | bytes 4276224 | tf_op jit(solution)/shard_map/back/pallas_call | solution.py:87
  84.4 3.1 %collective-permute-start.10 = (f32[15,64,128]{2,1,0:T(8,128)S(1)}, f32[15,64,128]{2,1,0:T(8,128)S(1)}, u32[]{:S(2)}, u32[]{:S(2)}) collective-permute-start(f32[15,64,128]{2,1,0:T(8,128)S(1)} %get-tuple-element.45), channel_id=1, source_target_pairs={{0,194},{4,198},{8,202},{12,206},{1,0},{5,4},{9,8},{13,12},{17,1},... | collective-permute-start | bytes 1474568 | tf_op jit(solution)/shard_map/layers_out/ppermute | solution.py:55
  87.5 2.7 %collective-permute-done.9.from_prev = f32[15,64,128]{2,1,0:T(8,128)S(1)} collective-permute-done((f32[15,64,128]{2,1,0:T(8,128)S(1)}, f32[15,64,128]{2,1,0:T(8,128)S(1)}, u32[]{:S(2)}, u32[]{:S(2)}) %collective-permute-start.9) | collective-permute-done | bytes 491552 | tf_op jit(solution)/shard_map/layers_out/ppermute | solution.py:55
  95.0 3.3 %collective-permute-done.12.from_next = f32[16,32,128]{2,1,0:T(8,128)S(1)} collective-permute-done((f32[16,32,128]{2,1,0:T(8,128)S(1)}, f32[16,32,128]{2,1,0:T(8,128)S(1)}, u32[]{:S(2)}, u32[]{:S(2)}) %collective-permute-start.12) | collective-permute-done | bytes 262176 | tf_op jit(solution)/shard_map/rows/ppermute | solution.py:60
  98.3 3.1 %collective-permute-done.11.from_prev = f32[16,32,128]{2,1,0:T(8,128)S(1)} collective-permute-done((f32[16,32,128]{2,1,0:T(8,128)S(1)}, f32[16,32,128]{2,1,0:T(8,128)S(1)}, u32[]{:S(2)}, u32[]{:S(2)}) %collective-permute-start.11) | collective-permute-done | bytes 262176 | tf_op jit(solution)/shard_map/rows/ppermute | solution.py:60
  102.3 5.3 %collective-permute-start.14 = (f32[16,64,128]{2,1,0:T(8,128)S(1)}, f32[16,64,128]{2,1,0:T(8,128)S(1)}, u32[]{:S(2)}, u32[]{:S(2)}) collective-permute-start(f32[16,64,128]{2,1,0:T(8,128)S(1)} %rows.5.own.ext), channel_id=1, source_target_pairs={{0,194},{4,198},{8,202},{12,206},{1,0},{5,4},{9,8},{13,12},{17,1},... | collective-permute-start | bytes 1572872 | tf_op jit(solution)/shard_map/layers_in/ppermute | solution.py:55
  107.6 2.9 %collective-permute-done.14.after = f32[16,64,128]{2,1,0:T(8,128)S(1)} collective-permute-done((f32[16,64,128]{2,1,0:T(8,128)S(1)}, f32[16,64,128]{2,1,0:T(8,128)S(1)}, u32[]{:S(2)}, u32[]{:S(2)}) %collective-permute-start.14) | collective-permute-done | bytes 524320 | tf_op jit(solution)/shard_map/layers_in/ppermute | solution.py:55
  110.4 3.3 %collective-permute-done.13.before = f32[16,64,128]{2,1,0:T(8,128)S(1)} collective-permute-done((f32[16,64,128]{2,1,0:T(8,128)S(1)}, f32[16,64,128]{2,1,0:T(8,128)S(1)}, u32[]{:S(2)}, u32[]{:S(2)}) %collective-permute-start.13) | collective-permute-done | bytes 524320 | tf_op jit(solution)/shard_map/layers_in/ppermute | solution.py:55
  113.7 4.5 %forward.3.fwd = f32[4,16,32,128]{3,2,1,0:T(8,128)S(1)} custom-call(f32[4,8,128]{2,1,0:T(8,128)S(1)} %get-tuple-element.34.taps, f32[16,64,128]{2,1,0:T(8,128)S(1)} %collective-permute-done.13.before, f32[16,64,128]{2,1,0:T(8,128)S(1)} %rows.5.own.ext, f32[16,64,128]{2,1,0:T(8,128)S(1)} %collective-permute-done.14.after, ...), custom_call_target="tpu_custom_call" | custom-call | flops 2000000000 | bytes 2179072 | tf_op jit(solution)/shard_map/forward/pallas_call | solution.py:87
  118.2 4.0 %back.3 = (f32[15,64,128]{2,1,0:T(8,128)S(1)}, f32[16,64,128]{2,1,0:T(8,128)S(1)}, f32[15,64,128]{2,1,0:T(8,128)S(1)}) custom-call(f32[4,8,128]{2,1,0:T(8,128)S(1)} %get-tuple-element.34.taps, f32[4,16,32,128]{3,2,1,0:T(8,128)S(1)} %forward.3.fwd, f32[4,16,32,128]{3,2,1,0:T(8,128)S(1)} %get-tuple-element.48.rec, ...), custom_call_target="tpu_custom_call" | custom-call | flops 2000000000 | bytes 2703360 | tf_op jit(solution)/shard_map/back/pallas_call | solution.py:87
  124.3 6.0 %collective-permute-start.16 = (f32[15,64,128]{2,1,0:T(8,128)S(1)}, f32[15,64,128]{2,1,0:T(8,128)S(1)}, u32[]{:S(2)}, u32[]{:S(2)}) collective-permute-start(f32[15,64,128]{2,1,0:T(8,128)S(1)} %get-tuple-element.51), channel_id=1, source_target_pairs={{0,194},{4,198},{8,202},{12,206},{1,0},{5,4},{9,8},{13,12},{17,1},... | collective-permute-start | bytes 1474568 | tf_op jit(solution)/shard_map/layers_out/ppermute | solution.py:55
  138.7 13.0 %collective-permute-start.19 = (f32[16,32,128]{2,1,0:T(8,128)S(1)}, f32[16,32,128]{2,1,0:T(8,128)S(1)}, u32[]{:S(2)}, u32[]{:S(2)}) collective-permute-start(f32[16,32,128]{2,1,0:T(8,128)S(1)} %rows.7), channel_id=1, source_target_pairs={{0,0},{1,4},{17,8},{16,12},{4,1},{5,5},{21,9},{20,13},{8,2},{9,6},... | collective-permute-start | bytes 786440 | tf_op jit(solution)/shard_map/result/ppermute | solution.py:46
  151.8 4.0 %collective-permute-done.19.c0 = f32[16,32,128]{2,1,0:T(8,128)S(1)} collective-permute-done((f32[16,32,128]{2,1,0:T(8,128)S(1)}, f32[16,32,128]{2,1,0:T(8,128)S(1)}, u32[]{:S(2)}, u32[]{:S(2)}) %collective-permute-start.19) | collective-permute-done | bytes 262176 | tf_op jit(solution)/shard_map/result/ppermute | solution.py:46
  155.8 5.8 %collective-permute-start.21 = (f32[16,32,128]{2,1,0:T(8,128)S(1)}, f32[16,32,128]{2,1,0:T(8,128)S(1)}, u32[]{:S(2)}, u32[]{:S(2)}) collective-permute-start(f32[16,32,128]{2,1,0:T(8,128)S(1)} %collective-permute-done.19.c0), channel_id=1, source_target_pairs={{0,2},{1,3},{2,0},{3,1},{4,6},{5,7},{6,4},{7,5},{8,10},{9,11},{10,... | collective-permute-start | bytes 786440 | tf_op jit(solution)/shard_map/result/ppermute | solution.py:50
  161.6 5.4 %collective-permute-done.21.c2 = f32[16,32,128]{2,1,0:T(8,128)S(1)} collective-permute-done((f32[16,32,128]{2,1,0:T(8,128)S(1)}, f32[16,32,128]{2,1,0:T(8,128)S(1)}, u32[]{:S(2)}, u32[]{:S(2)}) %collective-permute-start.21) | collective-permute-done | bytes 262176 | tf_op jit(solution)/shard_map/result/ppermute | solution.py:50
  (48 shorter events, 33.3 us)
Async XLA Ops:
  0.7 1.2 copy-start
  6.2 51.4 %collective-permute-start.4 = (f32[16,64,128]{2,1,0:T(8,128)S(1)}, f32[16,64,128]{2,1,0:T(8,128)S(1)}, u32[]{:S(2)}, u32[]{:S(2)}) collective-permute-start(f32[16,64,128]{2,1,0:T(8,128)S(1)} %get-tuple-element.35), channel_id=1, source_target_pairs={{0,0},{1,4},{2,8},{3,12},{4,1},{5,5},{6,9},{7,13},{8,17},{9,21},{1... | collective-permute-start | bytes 1572872 | tf_op jit(solution)/shard_map/spread/ppermute | solution.py:41
  10.7 31.4 %collective-permute-start = (f32[17,32,128]{2,1,0:T(8,128)S(1)}, f32[17,32,128]{2,1,0:T(8,128)S(1)}, u32[]{:S(2)}, u32[]{:S(2)}) collective-permute-start(f32[17,32,128]{2,1,0:T(8,128)S(1)} %get-tuple-element.30), channel_id=1, source_target_pairs={{0,0},{1,4},{2,8},{3,12},{4,1},{5,5},{6,9},{7,13},{8,17},{9,21},{1... | collective-permute-start | bytes 835592 | tf_op jit(solution)/shard_map/spread/ppermute | solution.py:41
  12.6 29.5 %collective-permute-start.1 = (f32[17,32,128]{2,1,0:T(8,128)S(1)}, f32[17,32,128]{2,1,0:T(8,128)S(1)}, u32[]{:S(2)}, u32[]{:S(2)}) collective-permute-start(f32[17,32,128]{2,1,0:T(8,128)S(1)} %get-tuple-element.31), channel_id=1, source_target_pairs={{0,4},{1,8},{2,12},{3,0},{4,5},{5,9},{6,13},{7,1},{8,21},{9,25},{1... | collective-permute-start | bytes 835592 | tf_op jit(solution)/shard_map/spread/ppermute | solution.py:41
  18.3 29.8 %collective-permute-start.2 = (f32[17,32,128]{2,1,0:T(8,128)S(1)}, f32[17,32,128]{2,1,0:T(8,128)S(1)}, u32[]{:S(2)}, u32[]{:S(2)}) collective-permute-start(f32[17,32,128]{2,1,0:T(8,128)S(1)} %get-tuple-element.32), channel_id=1, source_target_pairs={{0,8},{1,12},{2,0},{3,4},{4,9},{5,13},{6,1},{7,5},{8,25},{9,29},{1... | collective-permute-start | bytes 835592 | tf_op jit(solution)/shard_map/spread/ppermute | solution.py:41
  22.7 27.0 %collective-permute-start.3 = (f32[17,32,128]{2,1,0:T(8,128)S(1)}, f32[17,32,128]{2,1,0:T(8,128)S(1)}, u32[]{:S(2)}, u32[]{:S(2)}) collective-permute-start(f32[17,32,128]{2,1,0:T(8,128)S(1)} %get-tuple-element.33), channel_id=1, source_target_pairs={{0,12},{1,0},{2,4},{3,8},{4,13},{5,1},{6,5},{7,9},{8,29},{9,17},{1... | collective-permute-start | bytes 835592 | tf_op jit(solution)/shard_map/spread/ppermute | solution.py:41
  52.8 26.0 %collective-permute-start.7 = (f32[48,32,128]{2,1,0:T(8,128)S(1)}, f32[48,32,128]{2,1,0:T(8,128)S(1)}, u32[]{:S(2)}, u32[]{:S(2)}) collective-permute-start(f32[48,32,128]{2,1,0:T(8,128)S(1)} %get-tuple-element.39), channel_id=1, source_target_pairs={{0,1},{4,5},{8,9},{12,13},{1,17},{5,21},{9,25},{13,29},{17,16},{21... | collective-permute-start | bytes 2359304 | tf_op jit(solution)/shard_map/shift/ppermute | solution.py:55
  57.5 21.3 %collective-permute-start.8 = (f32[48,32,128]{2,1,0:T(8,128)S(1)}, f32[48,32,128]{2,1,0:T(8,128)S(1)}, u32[]{:S(2)}, u32[]{:S(2)}) collective-permute-start(f32[48,32,128]{2,1,0:T(8,128)S(1)} %get-tuple-element.40), channel_id=1, source_target_pairs={{0,194},{4,198},{8,202},{12,206},{1,0},{5,4},{9,8},{13,12},{17,1},... | collective-permute-start | bytes 2359304 | tf_op jit(solution)/shard_map/shift/ppermute | solution.py:55
  57.5 16.7 %collective-permute-start.6 = (f32[16,64,128]{2,1,0:T(8,128)S(1)}, f32[16,64,128]{2,1,0:T(8,128)S(1)}, u32[]{:S(2)}, u32[]{:S(2)}) collective-permute-start(f32[16,64,128]{2,1,0:T(8,128)S(1)} %collective-permute-done.4.own.ext), channel_id=1, source_target_pairs={{0,194},{4,198},{8,202},{12,206},{1,0},{5,4},{9,8},{13,12},{17,1},... | collective-permute-start | bytes 1572872 | tf_op jit(solution)/shard_map/layers_in/ppermute | solution.py:55
  61.5 12.8 %collective-permute-start.5 = (f32[16,64,128]{2,1,0:T(8,128)S(1)}, f32[16,64,128]{2,1,0:T(8,128)S(1)}, u32[]{:S(2)}, u32[]{:S(2)}) collective-permute-start(f32[16,64,128]{2,1,0:T(8,128)S(1)} %collective-permute-done.4.own.ext), channel_id=1, source_target_pairs={{0,1},{4,5},{8,9},{12,13},{1,17},{5,21},{9,25},{13,29},{17,16},{21... | collective-permute-start | bytes 1572872 | tf_op jit(solution)/shard_map/layers_in/ppermute | solution.py:55
  84.3 5.9 %collective-permute-start.9 = (f32[15,64,128]{2,1,0:T(8,128)S(1)}, f32[15,64,128]{2,1,0:T(8,128)S(1)}, u32[]{:S(2)}, u32[]{:S(2)}) collective-permute-start(f32[15,64,128]{2,1,0:T(8,128)S(1)} %get-tuple-element.44), channel_id=1, source_target_pairs={{0,1},{4,5},{8,9},{12,13},{1,17},{5,21},{9,25},{13,29},{17,16},{21... | collective-permute-start | bytes 1474568 | tf_op jit(solution)/shard_map/layers_out/ppermute | solution.py:55
  84.4 8.2 %collective-permute-start.10 = (f32[15,64,128]{2,1,0:T(8,128)S(1)}, f32[15,64,128]{2,1,0:T(8,128)S(1)}, u32[]{:S(2)}, u32[]{:S(2)}) collective-permute-start(f32[15,64,128]{2,1,0:T(8,128)S(1)} %get-tuple-element.45), channel_id=1, source_target_pairs={{0,194},{4,198},{8,202},{12,206},{1,0},{5,4},{9,8},{13,12},{17,1},... | collective-permute-start | bytes 1474568 | tf_op jit(solution)/shard_map/layers_out/ppermute | solution.py:55
  92.8 5.5 %collective-permute-start.12 = (f32[16,32,128]{2,1,0:T(8,128)S(1)}, f32[16,32,128]{2,1,0:T(8,128)S(1)}, u32[]{:S(2)}, u32[]{:S(2)}) collective-permute-start(f32[16,32,128]{2,1,0:T(8,128)S(1)} %get-tuple-element.46.low), channel_id=1, source_target_pairs={{0,12},{4,0},{8,4},{12,8},{1,13},{5,1},{9,5},{13,9},{17,29},{21,17... | collective-permute-start | bytes 786440 | tf_op jit(solution)/shard_map/rows/ppermute | solution.py:60
  95.0 6.4 %collective-permute-start.11 = (f32[16,32,128]{2,1,0:T(8,128)S(1)}, f32[16,32,128]{2,1,0:T(8,128)S(1)}, u32[]{:S(2)}, u32[]{:S(2)}) collective-permute-start(f32[16,32,128]{2,1,0:T(8,128)S(1)} %get-tuple-element.47.high), channel_id=1, source_target_pairs={{0,4},{4,8},{8,12},{12,0},{1,5},{5,9},{9,13},{13,1},{17,21},{21,25... | collective-permute-start | bytes 786440 | tf_op jit(solution)/shard_map/rows/ppermute | solution.py:60
  102.3 8.1 %collective-permute-start.14 = (f32[16,64,128]{2,1,0:T(8,128)S(1)}, f32[16,64,128]{2,1,0:T(8,128)S(1)}, u32[]{:S(2)}, u32[]{:S(2)}) collective-permute-start(f32[16,64,128]{2,1,0:T(8,128)S(1)} %rows.5.own.ext), channel_id=1, source_target_pairs={{0,194},{4,198},{8,202},{12,206},{1,0},{5,4},{9,8},{13,12},{17,1},... | collective-permute-start | bytes 1572872 | tf_op jit(solution)/shard_map/layers_in/ppermute | solution.py:55
  107.6 6.1 %collective-permute-start.13 = (f32[16,64,128]{2,1,0:T(8,128)S(1)}, f32[16,64,128]{2,1,0:T(8,128)S(1)}, u32[]{:S(2)}, u32[]{:S(2)}) collective-permute-start(f32[16,64,128]{2,1,0:T(8,128)S(1)} %rows.5.own.ext), channel_id=1, source_target_pairs={{0,1},{4,5},{8,9},{12,13},{1,17},{5,21},{9,25},{13,29},{17,16},{21... | collective-permute-start | bytes 1572872 | tf_op jit(solution)/shard_map/layers_in/ppermute | solution.py:55
  122.3 9.2 %collective-permute-start.15 = (f32[15,64,128]{2,1,0:T(8,128)S(1)}, f32[15,64,128]{2,1,0:T(8,128)S(1)}, u32[]{:S(2)}, u32[]{:S(2)}) collective-permute-start(f32[15,64,128]{2,1,0:T(8,128)S(1)} %get-tuple-element.50), channel_id=1, source_target_pairs={{0,1},{4,5},{8,9},{12,13},{1,17},{5,21},{9,25},{13,29},{17,16},{21... | collective-permute-start | bytes 1474568 | tf_op jit(solution)/shard_map/layers_out/ppermute | solution.py:55
  124.3 7.7 %collective-permute-start.16 = (f32[15,64,128]{2,1,0:T(8,128)S(1)}, f32[15,64,128]{2,1,0:T(8,128)S(1)}, u32[]{:S(2)}, u32[]{:S(2)}) collective-permute-start(f32[15,64,128]{2,1,0:T(8,128)S(1)} %get-tuple-element.51), channel_id=1, source_target_pairs={{0,194},{4,198},{8,202},{12,206},{1,0},{5,4},{9,8},{13,12},{17,1},... | collective-permute-start | bytes 1474568 | tf_op jit(solution)/shard_map/layers_out/ppermute | solution.py:55
  132.1 5.4 %collective-permute-start.17 = (f32[16,16,128]{2,1,0:T(8,128)S(1)}, f32[16,16,128]{2,1,0:T(8,128)S(1)}, u32[]{:S(2)}, u32[]{:S(2)}) collective-permute-start(f32[16,16,128]{2,1,0:T(8,128)S(1)} %get-tuple-element.53), channel_id=1, source_target_pairs={{0,4},{4,8},{8,12},{12,0},{1,5},{5,9},{9,13},{13,1},{17,21},{21,25... | collective-permute-start | bytes 393224 | tf_op jit(solution)/shard_map/rows/ppermute | solution.py:60
  133.5 4.3 %collective-permute-start.18 = (f32[16,16,128]{2,1,0:T(8,128)S(1)}, f32[16,16,128]{2,1,0:T(8,128)S(1)}, u32[]{:S(2)}, u32[]{:S(2)}) collective-permute-start(f32[16,16,128]{2,1,0:T(8,128)S(1)} %get-tuple-element.54), channel_id=1, source_target_pairs={{0,12},{4,0},{8,4},{12,8},{1,13},{5,1},{9,5},{13,9},{17,29},{21,17... | collective-permute-start | bytes 393224 | tf_op jit(solution)/shard_map/rows/ppermute | solution.py:60
  138.7 17.1 %collective-permute-start.19 = (f32[16,32,128]{2,1,0:T(8,128)S(1)}, f32[16,32,128]{2,1,0:T(8,128)S(1)}, u32[]{:S(2)}, u32[]{:S(2)}) collective-permute-start(f32[16,32,128]{2,1,0:T(8,128)S(1)} %rows.7), channel_id=1, source_target_pairs={{0,0},{1,4},{17,8},{16,12},{4,1},{5,5},{21,9},{20,13},{8,2},{9,6},... | collective-permute-start | bytes 786440 | tf_op jit(solution)/shard_map/result/ppermute | solution.py:46
  155.8 11.2 %collective-permute-start.21 = (f32[16,32,128]{2,1,0:T(8,128)S(1)}, f32[16,32,128]{2,1,0:T(8,128)S(1)}, u32[]{:S(2)}, u32[]{:S(2)}) collective-permute-start(f32[16,32,128]{2,1,0:T(8,128)S(1)} %collective-permute-done.19.c0), channel_id=1, source_target_pairs={{0,2},{1,3},{2,0},{3,1},{4,6},{5,7},{6,4},{7,5},{8,10},{9,11},{10,... | collective-permute-start | bytes 786440 | tf_op jit(solution)/shard_map/result/ppermute | solution.py:50
  161.6 5.4 %collective-permute-start.20 = (f32[16,32,128]{2,1,0:T(8,128)S(1)}, f32[16,32,128]{2,1,0:T(8,128)S(1)}, u32[]{:S(2)}, u32[]{:S(2)}) collective-permute-start(f32[16,32,128]{2,1,0:T(8,128)S(1)} %collective-permute-done.19.c0), channel_id=1, source_target_pairs={{0,1},{1,0},{2,3},{3,2},{4,5},{5,4},{6,7},{7,6},{8,9},{9,8},{10,11... | collective-permute-start | bytes 786440 | tf_op jit(solution)/shard_map/result/ppermute | solution.py:50
  167.0 1.5 collective-permute-start.22
  (6 other events, 5.0 us)

commit v2 on v1

--- a/solution.py
+++ b/solution.py
@@ -11,6 +11,7 @@
 VIEWS = 4
 BZ = 16
 ROWS = 32
+FLAT = BZ * ROWS
 EXT = 64
 LANES = 128
 EDGE = 16
@@ -36,13 +37,20 @@
     return device(z, y, r, 2 * z_lo + (core ^ (chip % 2)))
 
 
+FAR = (1, 3, 0, 2)
+
+
+def quarter_of(q, v, j):
+    return (q + FAR[v ^ j]) % 4
+
+
 def spread(x, j):
-    perm = [(device(z, y, c, v), place(16 * z + 4 * y + c, (v + j) % 4)) for z, y, c, v in CELLS]
+    perm = [(device(z, y, q, v), place(16 * z + 4 * y + q, quarter_of(q, v, j))) for z, y, q, v in CELLS]
     return lax.ppermute(x, AXES, perm)
 
 
 def collect(x, j):
-    perm = [(place(16 * z + 4 * y + q, r), device(z, y, q, (r + j) % 4)) for z, y, r, q in CELLS]
+    perm = [(place(16 * z + 4 * y + q, quarter_of(q, v, j)), device(z, y, q, v)) for z, y, q, v in CELLS]
     return lax.ppermute(x, AXES, perm)
 
 
@@ -70,6 +78,19 @@
     return view, lax.rem(blk, 4), lax.div(blk, 16) * 16 + 2 * chip + core
 
 
+def quarter_at(j):
+    q = lax.rem(lax.axis_index("blk"), 4)
+    slot = lax.axis_index("view") ^ j
+    far = jnp.where(slot == 0, 1, jnp.where(slot == 1, 3, jnp.where(slot == 2, 0, 2)))
+    return lax.rem(q + far, 4)
+
+
+def view_at(j):
+    _, r, block = position()
+    far = lax.rem(r - lax.rem(block, 4) + 4, 4)
+    return jnp.where(far == 1, 0, jnp.where(far == 3, 1, jnp.where(far == 0, 2, 3))) ^ j
+
+
 def vmem():
     return pl.BlockSpec(memory_space=pltpu.VMEM)
 
@@ -82,7 +103,7 @@
     return pl.BlockSpec(memory_space=pl.ANY)
 
 
-def call(body, outs, args, specs, scratch, flops, out_specs=None):
+def call(body, outs, args, specs, scratch, flops, out_specs=None, mib=48):
     size = sum(a.size * a.dtype.itemsize for a in args)
     return pl.pallas_call(
         body,
@@ -90,7 +111,7 @@
         in_specs=specs,
         out_specs=out_specs or jax.tree.map(lambda _: vmem(), outs),
         scratch_shapes=scratch,
-        compiler_params=pltpu.CompilerParams(vmem_limit_bytes=48 * 1024 * 1024),
+        compiler_params=pltpu.CompilerParams(vmem_limit_bytes=mib * 1024 * 1024),
         cost_estimate=pl.CostEstimate(flops=flops, bytes_accessed=size, transcendentals=0),
     )(*args)
 
@@ -109,16 +130,7 @@
     return high, low
 
 
-def prologue_body(offsets, weight, est, rec, psf_z, psf_y, psf_x, ext, o0, o1, o2, o3, held, moved, sems, sem):
-    view = lax.axis_index("view")
-    step = BZ // 4
-    parts = [
-        pltpu.make_async_copy(rec.at[0, pl.ds(k * step, step)], held.at[pl.ds(k * step, step)], sems.at[k])
-        for k in range(4)
-    ]
-    for part in parts:
-        part.start()
-
+def start_body(est, ext, sem):
     def window(k):
         first = max(0, k * ROWS - EDGE)
         size = min(LANES, (k + 1) * ROWS + EDGE) - first
@@ -127,14 +139,17 @@
 
     for k in range(VIEWS):
 
-        @pl.when(view == k)
+        @pl.when(quarter_at(0) == k)
         def _(k=k):
             window(k).start()
             if k == 0:
                 ext[:, :EDGE, :] = jnp.zeros((BZ, EDGE, LANES), F32)
             if k == VIEWS - 1:
                 ext[:, EXT - EDGE :, :] = jnp.zeros((BZ, EDGE, LANES), F32)
-
+            window(k).wait()
+
+
+def planes_body(offsets, weight, rec, psf_z, psf_y, psf_x, o0, o1, o2, o3, moved):
     dy, dx = offsets[0, 1], offsets[0, 2]
     row = iota((LANES, LANES), 0) + dy
     col = iota((LANES, LANES), 1) + dx
@@ -142,69 +157,53 @@
     back_y = lax.rem(LANES - dy, LANES)
     back_x = lax.rem(LANES - dx, LANES)
 
-    for k, part in enumerate(parts):
-        part.wait()
-
-        @pl.loop(k * step, (k + 1) * step)
-        def _(z):
-            plane = pltpu.roll(pltpu.roll(held[z], back_y, 0), back_x, 1)
-            moved[z] = jnp.where(inside, plane, 0.0)
+    @pl.loop(0, BZ)
+    def _(z):
+        plane = pltpu.roll(pltpu.roll(rec[0, z], back_y, 0), back_x, 1)
+        moved[z] = jnp.where(inside, plane, 0.0)
 
     hz, hy, hx = (t[...] / jnp.sum(t[...], axis=1, keepdims=True) for t in (psf_z, psf_y, psf_x))
     lane = iota((1, LANES), 1)
     misc = jnp.where(lane == 0, weight[0], jnp.where(lane == 1, offsets[0, 0].astype(F32), 0.0))
     for j, out in enumerate((o0, o1, o2, o3)):
-        start = pl.multiple_of(lax.rem(view + j, VIEWS) * ROWS, ROWS)
-        out[:BZ] = moved[:, pl.ds(start, ROWS), :]
-        out[BZ] = jnp.zeros((ROWS, LANES), F32)
-        out[BZ, HZ : HZ + 1, :TAPS] = hz
-        out[BZ, HY : HY + 1, :TAPS] = hy
-        out[BZ, HX : HX + 1, :TAPS] = hx
-        out[BZ, WZ : WZ + 1, :TAPS] = weight[0] * hz
-        out[BZ, MISC : MISC + 1, :] = misc
-
-    for k in range(VIEWS):
-
-        @pl.when(view == k)
-        def _(k=k):
-            window(k).wait()
+        start = pl.multiple_of(quarter_at(j) * ROWS, ROWS)
+        out[:FLAT] = moved[:, pl.ds(start, ROWS), :].reshape(FLAT, LANES)
+        out[FLAT:] = jnp.zeros((8, LANES), F32)
+        for row, value in ((HZ, hz), (HY, hy), (HX, hx), (WZ, weight[0] * hz)):
+            out[FLAT + row : FLAT + row + 1, :TAPS] = value
+        out[FLAT + MISC : FLAT + MISC + 1, :] = misc
 
 
 def shift_of(taps, v):
     return taps[v, MISC, 1].astype(jnp.int32)
 
 
-def pack_body(a0, a1, a2, a3, up, down, rec, taps, held, sems, tap_sems):
+def pack_body(a0, a1, a2, a3, up, down, taps, held, sems, tap_sems):
     blocks = (a0, a1, a2, a3)
-    data = [pltpu.make_async_copy(a.at[pl.ds(0, BZ)], held.at[v], sems.at[v]) for v, a in enumerate(blocks)]
-    rows = [
-        pltpu.make_async_copy(a.at[BZ, pl.ds(0, 8)], taps.at[v], tap_sems.at[v]) for v, a in enumerate(blocks)
-    ]
+    data, rows = [], []
+    for j, a in enumerate(blocks):
+        data.append(pltpu.make_async_copy(a.at[pl.ds(0, FLAT)], held.at[view_at(j)], sems.at[j]))
+        rows.append(pltpu.make_async_copy(a.at[pl.ds(FLAT, 8)], taps.at[view_at(j)], tap_sems.at[j]))
     for copy in rows + data:
         copy.start()
+    for copy in rows + data:
+        copy.wait()
     for out in (up, down):
-        out[BZ:] = jnp.zeros((2 * BZ, ROWS, LANES), F32)
+        out[FLAT:] = jnp.zeros((2 * FLAT, LANES), F32)
     n_up, n_down = jnp.int32(0), jnp.int32(0)
     for v in range(VIEWS):
-        rows[v].wait()
-        data[v].wait()
         dz = shift_of(taps, v)
 
         @pl.when(dz < 0)
         def _(v=v, n=n_up):
-            up[pl.ds(n * BZ, BZ)] = held[v]
+            up[pl.ds(pl.multiple_of(n * FLAT, FLAT), FLAT)] = held[v]
 
         @pl.when(dz > 0)
         def _(v=v, n=n_down):
-            down[pl.ds(n * BZ, BZ)] = held[v]
+            down[pl.ds(pl.multiple_of(n * FLAT, FLAT), FLAT)] = held[v]
 
         n_up = n_up + jnp.where(dz < 0, 1, 0)
         n_down = n_down + jnp.where(dz > 0, 1, 0)
-
-        @pl.loop(0, BZ)
-        def _(i, v=v, dz=dz):
-            src = i + dz
-            rec[v, i] = jnp.where((src >= 0) & (src < BZ), held[v, jnp.clip(src, 0, BZ - 1)], 0.0)
 
 
 def bands_body(taps, wy_f, wy_b, wx_f, wx_b):
@@ -261,46 +260,54 @@
             inner[v, 2 * p] = rows[:, :LANES]
             inner[v, 2 * p + 1] = rows[:, LANES:]
 
-    @pl.loop(0, VIEWS * 4)
-    def _(n):
-        v = lax.div(n, 4)
-        rows = pl.ds(pl.multiple_of(lax.rem(n, 4) * 8, 8), 8)
+    def sum_z(v):
         hz = [taps[v, HZ, a] for a in range(TAPS)]
-        acc = [None] * BZ
-        for k in range(LAYERS):
-            x = inner[v, k, rows, :]
-            for i in range(max(0, k - TAPS + 1), min(BZ - 1, k) + 1):
-                term = hz[k - i] * x
-                acc[i] = term if acc[i] is None else acc[i] + term
-        for i in range(BZ):
-            summed[v, i, rows, :] = acc[i]
-
-    for v in range(VIEWS):
+        for t in range(ROWS // 8):
+            rows = slice(8 * t, 8 * t + 8)
+            acc = [None] * BZ
+            for k in range(LAYERS):
+                x = inner[v, k, rows, :]
+                for i in range(max(0, k - TAPS + 1), min(BZ - 1, k) + 1):
+                    term = hz[k - i] * x
+                    acc[i] = term if acc[i] is None else acc[i] + term
+            for i in range(BZ):
+                summed[v, i, rows, :] = acc[i]
+
+    def mix_x(v):
         high, low = pieces(summed[v].reshape(BZ * ROWS, LANES))
         done = jnp.dot(jnp.concatenate([high, low], 1), wx_f[v], preferred_element_type=F32)
         out[v] = (done[:, :LANES] + done[:, LANES:]).reshape(BZ, ROWS, LANES)
 
+    for v in range(VIEWS):
+        sum_z(v)
+        if v > 0:
+            mix_x(v - 1)
+    mix_x(VIEWS - 1)
+
 
 def back_body(taps, fwd, rec, wx_b, wy_b, before, own, after, inner, spread_z):
-    for v in range(VIEWS):
+    def mix_x(v):
         ratio = (rec[v] / fwd[v]).reshape(BZ * ROWS, LANES)
         high, low = pieces(ratio)
         done = jnp.dot(jnp.concatenate([high, low], 1), wx_b[v], preferred_element_type=F32)
         inner[v] = (done[:, :LANES] + done[:, LANES:]).reshape(BZ, ROWS, LANES)
 
-    @pl.loop(0, VIEWS * 4)
-    def _(n):
-        v = lax.div(n, 4)
-        rows = pl.ds(pl.multiple_of(lax.rem(n, 4) * 8, 8), 8)
-        place_rows = pl.ds(pl.multiple_of(n * 8, 8), 8)
+    def spread_layers(v):
         hz = [taps[v, WZ, a] for a in range(TAPS)]
-        x = [inner[v, i, rows, :] for i in range(BZ)]
-        for k in range(LAYERS):
-            acc = None
-            for i in range(max(0, k - TAPS + 1), min(BZ - 1, k) + 1):
-                term = hz[k - i] * x[i]
-                acc = term if acc is None else acc + term
-            spread_z[k, place_rows, :] = acc
+        for t in range(ROWS // 8):
+            x = [inner[v, i, 8 * t : 8 * t + 8, :] for i in range(BZ)]
+            for k in range(LAYERS):
+                acc = None
+                for i in range(max(0, k - TAPS + 1), min(BZ - 1, k) + 1):
+                    term = hz[k - i] * x[i]
+                    acc = term if acc is None else acc + term
+                spread_z[k, v * ROWS + 8 * t : v * ROWS + 8 * t + 8, :] = acc
+
+    mix_x(0)
+    for v in range(VIEWS):
+        if v < VIEWS - 1:
+            mix_x(v + 1)
+        spread_layers(v)
 
     def store(k, value):
         if k < HALF:
@@ -318,10 +325,12 @@
         store(2 * p + 1, both[:, LANES:])
 
 
-def first_back_body(taps, fwd, part, lower, upper, wx_b, wy_b, *rest):
-    before, own, after, rec, low, high, sems, inner, spread_z = rest
+def first_back_body(taps, fwd, a0, a1, a2, a3, lower, upper, wx_b, wy_b, *rest):
+    before, own, after, rec, held, low, high, sems, inner, spread_z = rest
     _, _, block = position()
-    copies = [pltpu.make_async_copy(lower, low, sems.at[0]), pltpu.make_async_copy(upper, high, sems.at[1])]
+    copies = [pltpu.make_async_copy(lower, low, sems.at[4]), pltpu.make_async_copy(upper, high, sems.at[5])]
+    for j, a in enumerate((a0, a1, a2, a3)):
+        copies.append(pltpu.make_async_copy(a.at[pl.ds(0, FLAT)], held.at[view_at(j)], sems.at[j]))
     for copy in copies:
         copy.start()
     for copy in copies:
@@ -334,9 +343,13 @@
         def _(i, v=v, dz=dz, n_up=n_up, n_down=n_down):
             src = i + dz
             place_z = block * BZ + src
-            x = part[v, i]
-            x = jnp.where(src < 0, low[jnp.clip(n_up * BZ + src + BZ, 0, 3 * BZ - 1)], x)
-            x = jnp.where(src >= BZ, high[jnp.clip(n_down * BZ + src - BZ, 0, 3 * BZ - 1)], x)
+
+            def rows(layer, count):
+                return pl.ds(pl.multiple_of(jnp.clip(layer, 0, count - 1) * ROWS, ROWS), ROWS)
+
+            x = held[v, rows(src, BZ), :]
+            x = jnp.where(src < 0, low[rows(n_up * BZ + src + BZ, 3 * BZ), :], x)
+            x = jnp.where(src >= BZ, high[rows(n_down * BZ + src - BZ, 3 * BZ), :], x)
             rec[v, i] = jnp.where((place_z >= 0) & (place_z < 64 * BZ), x, 0.0)
 
         n_up = n_up + jnp.where(dz < 0, 1, 0)
@@ -396,9 +409,8 @@
 
 
 def join_body(c0, c1, c2, c3, out):
-    view = lax.axis_index("view")
     for mask, chunk in enumerate((c0, c1, c2, c3)):
-        start = pl.multiple_of((view ^ mask) * ROWS, ROWS)
+        start = pl.multiple_of(quarter_at(mask) * ROWS, ROWS)
         out[:, pl.ds(start, ROWS), :] = chunk[...]
 
 
@@ -408,37 +420,37 @@
 WINDOW = (BZ, EXT, LANES)
 HALO = (HALF, EXT, LANES)
 QUARTER = (BZ, ROWS, LANES)
-PACKED = (3 * BZ, ROWS, LANES)
+PACKED = (3 * FLAT, LANES)
 STRIP = (BZ, EDGE, LANES)
 
 
 def per_device(estimate, recorded, offsets, psf_z, psf_y, psf_x, view_weights):
-    with jax.named_scope("prologue"):
-        ext, *chunks = call(
-            prologue_body,
-            (shape(*WINDOW),) + (shape(BZ + 1, ROWS, LANES),) * 4,
-            (offsets, view_weights, estimate, recorded, psf_z, psf_y, psf_x),
-            [smem(), smem(), hbm(), hbm()] + [vmem()] * 3,
-            [
-                pltpu.VMEM((BZ, LANES, LANES), F32),
-                pltpu.VMEM((BZ, LANES, LANES), F32),
-                pltpu.SemaphoreType.DMA((4,)),
-                pltpu.SemaphoreType.DMA,
-            ],
+    with jax.named_scope("window"):
+        ext = call(start_body, shape(*WINDOW), (estimate,), [hbm()], [pltpu.SemaphoreType.DMA], 1_000_000)
+        ext = spread(ext, 0)
+    with jax.named_scope("planes"):
+        chunks = call(
+            planes_body,
+            (shape(FLAT + 8, LANES),) * 4,
+            (offsets, view_weights, recorded, psf_z, psf_y, psf_x),
+            [smem(), smem()] + [vmem()] * 4,
+            [pltpu.VMEM((BZ, LANES, LANES), F32)],
             10_000_000,
         )
     with jax.named_scope("spread"):
-        ext = spread(ext, 0)
         mine = [spread(c, j) for j, c in enumerate(chunks)]
+    with jax.named_scope("layers_in"):
+        before = to_layer(ext, 1)
+        after = to_layer(ext, -1)
     with jax.named_scope("shift"):
-        up, down, part, taps = call(
+        up, down, taps = call(
             pack_body,
-            (shape(*PACKED), shape(*PACKED), shape(*BLOCK), shape(VIEWS, 8, LANES)),
+            (shape(*PACKED), shape(*PACKED), shape(VIEWS, 8, LANES)),
             tuple(mine),
             [hbm()] * 4,
-            [pltpu.VMEM(BLOCK, F32), pltpu.SemaphoreType.DMA((4,)), pltpu.SemaphoreType.DMA((4,))],
-            10_000_000,
-            (vmem(), vmem(), vmem(), smem()),
+            [pltpu.VMEM((VIEWS, FLAT, LANES), F32), pltpu.SemaphoreType.DMA((4,)), pltpu.SemaphoreType.DMA((4,))],
+            8_000_000_000,
+            (vmem(), vmem(), smem()),
         )
         lower = to_layer(up, 1)
         upper = to_layer(down, -1)
@@ -460,9 +472,10 @@
 
     rec = None
     for step in range(ITERS):
-        with jax.named_scope("layers_in"):
-            before = to_layer(ext, 1)
-            after = to_layer(ext, -1)
+        if step > 0:
+            with jax.named_scope("layers_in"):
+                before = to_layer(ext, 1)
+                after = to_layer(ext, -1)
         with jax.named_scope("forward"):
             fwd = call(
                 forward_body,
@@ -470,7 +483,7 @@
                 (taps, before, ext, after, wy_f, wx_f),
                 [smem()] + [vmem()] * 5,
                 [pltpu.VMEM(INNER, F32), pltpu.VMEM(BLOCK, F32)],
-                2_000_000_000,
+                20_000_000_000 if step == 0 else 2_000_000_000,
             )
         with jax.named_scope("back"):
             outs = (shape(*HALO), shape(*WINDOW), shape(*HALO))
@@ -479,9 +492,15 @@
                 c_before, c_own, c_after, rec = call(
                     first_back_body,
                     outs + (shape(*BLOCK),),
-                    (taps, fwd, part, lower, upper, wx_b, wy_b),
-                    [smem(), vmem(), vmem(), hbm(), hbm(), vmem(), vmem()],
-                    [pltpu.VMEM(PACKED, F32), pltpu.VMEM(PACKED, F32), pltpu.SemaphoreType.DMA((2,))] + scratch,
+                    (taps, fwd, *mine, lower, upper, wx_b, wy_b),
+                    [smem(), vmem()] + [hbm()] * 6 + [vmem()] * 2,
+                    [
+                        pltpu.VMEM((VIEWS, FLAT, LANES), F32),
+                        pltpu.VMEM(PACKED, F32),
+                        pltpu.VMEM(PACKED, F32),
+                        pltpu.SemaphoreType.DMA((6,)),
+                    ]
+                    + scratch,
                     2_000_000_000,
                 )
             else:
@@ -535,7 +554,7 @@
     with jax.named_scope("result"):
         c0 = collect(own, 0)
         c1 = view_swap(c0, 1)
-        c2 = view_swap(c0, 2)
+        c2 = collect(own, 2)
         c3 = view_swap(c2, 1)
         return call(join_body, shape(BZ, LANES, LANES), (c0, c1, c2, c3), [vmem()] * 4, [], 1_000_000)
 

time: 170 us -> 150 us (0.88)
  the two profiles are of different devices: /device:TPU:1 before, /device:TPU:95 now
where the time goes in v2:
time: 150 us; the launch traced here: 149 us
  waiting for transfers between devices  73.4 us (49%)
  starting transfers between devices  46.1 us (31%)
  Pallas kernels  26.5 us (18%)
  local copies, waits for them, and re-layouts  2.24 us (1%)
    pallas_call x13, Pallas kernels, call(): pl.pallas_call(body, out_shape=outs, in_specs=specs, out_specs=out_specs...  26.5 us
    ppermute x10, waiting for transfers between devices, to_layer(): return lax.ppermute(x, AXES, perm)  25.5 us
    ppermute x2, waiting for transfers between devices, collect(): return lax.ppermute(x, AXES, perm)  20.3 us
    ppermute x5, starting transfers between devices, spread(): return lax.ppermute(x, AXES, perm)  19.1 us
    ppermute x5, waiting for transfers between devices, spread(): return lax.ppermute(x, AXES, perm)  17.7 us
    ppermute x2, starting transfers between devices, collect(): return lax.ppermute(x, AXES, perm)  10.3 us
    ppermute x10, starting transfers between devices, to_layer(): return lax.ppermute(x, AXES, perm)  9.66 us
    ppermute x4, waiting for transfers between devices, to_row(): return lax.ppermute(x, AXES, perm)  8.78 us
  transfers between devices with their start and end apart: 23, of which 15 were waited for; matrix products, arithmetic and copies ran while one was open for 0% of the time, Pallas kernels for 7%

profile of v2, /device:TPU:95, one launch (start us, length us, event | category | flops | bytes accessed | tf_op | source)
XLA Modules:
  0.0 149.2 jit_solution(1422249982770499878)
XLA Ops:
  1.3 4.2 %collective-permute-start.4 = (f32[16,64,128]{2,1,0:T(8,128)S(1)}, f32[16,64,128]{2,1,0:T(8,128)S(1)}, u32[]{:S(2)}, u32[]{:S(2)}) collective-permute-start(f32[16,64,128]{2,1,0:T(8,128)S(1)} %window.1), channel_id=1, source_target_pairs={{0,4},{1,12},{2,0},{3,8},{4,9},{5,1},{6,5},{7,13},{8,29},{9,21},{1... | collective-permute-start | bytes 1572872 | tf_op jit(solution)/shard_map/window/ppermute | solution.py:49
  8.4 2.5 %collective-permute-start = (f32[520,128]{1,0:T(8,128)S(1)}, f32[520,128]{1,0:T(8,128)S(1)}, u32[]{:S(2)}, u32[]{:S(2)}) collective-permute-start(f32[520,128]{1,0:T(8,128)S(1)} %get-tuple-element.28), channel_id=1, source_target_pairs={{0,4},{1,12},{2,0},{3,8},{4,9},{5,1},{6,5},{7,13},{8,29},{9,21},{1... | collective-permute-start | bytes 798728 | tf_op jit(solution)/shard_map/spread/ppermute | solution.py:49
  10.8 2.6 %collective-permute-start.1 = (f32[520,128]{1,0:T(8,128)S(1)}, f32[520,128]{1,0:T(8,128)S(1)}, u32[]{:S(2)}, u32[]{:S(2)}) collective-permute-start(f32[520,128]{1,0:T(8,128)S(1)} %get-tuple-element.29), channel_id=1, source_target_pairs={{0,12},{1,4},{2,8},{3,0},{4,1},{5,9},{6,13},{7,5},{8,21},{9,29},{1... | collective-permute-start | bytes 798728 | tf_op jit(solution)/shard_map/spread/ppermute | solution.py:49
  13.4 7.5 %collective-permute-start.2 = (f32[520,128]{1,0:T(8,128)S(1)}, f32[520,128]{1,0:T(8,128)S(1)}, u32[]{:S(2)}, u32[]{:S(2)}) collective-permute-start(f32[520,128]{1,0:T(8,128)S(1)} %get-tuple-element.30), channel_id=1, source_target_pairs={{0,0},{1,8},{2,4},{3,12},{4,5},{5,13},{6,9},{7,1},{8,25},{9,17},{1... | collective-permute-start | bytes 798728 | tf_op jit(solution)/shard_map/spread/ppermute | solution.py:49
  20.9 2.4 %collective-permute-start.3 = (f32[520,128]{1,0:T(8,128)S(1)}, f32[520,128]{1,0:T(8,128)S(1)}, u32[]{:S(2)}, u32[]{:S(2)}) collective-permute-start(f32[520,128]{1,0:T(8,128)S(1)} %get-tuple-element.31), channel_id=1, source_target_pairs={{0,8},{1,0},{2,12},{3,4},{4,13},{5,5},{6,1},{7,9},{8,17},{9,25},{1... | collective-permute-start | bytes 798728 | tf_op jit(solution)/shard_map/spread/ppermute | solution.py:49
  23.4 8.1 %collective-permute-done.a0 = f32[520,128]{1,0:T(8,128)S(1)} collective-permute-done((f32[520,128]{1,0:T(8,128)S(1)}, f32[520,128]{1,0:T(8,128)S(1)}, u32[]{:S(2)}, u32[]{:S(2)}) %collective-permute-start) | collective-permute-done | bytes 266272 | tf_op jit(solution)/shard_map/spread/ppermute | solution.py:49
  31.6 5.1 %collective-permute-done.2.a2 = f32[520,128]{1,0:T(8,128)S(1)} collective-permute-done((f32[520,128]{1,0:T(8,128)S(1)}, f32[520,128]{1,0:T(8,128)S(1)}, u32[]{:S(2)}, u32[]{:S(2)}) %collective-permute-start.2) | collective-permute-done | bytes 266272 | tf_op jit(solution)/shard_map/spread/ppermute | solution.py:49
  36.7 4.5 %collective-permute-done.3.a3 = f32[520,128]{1,0:T(8,128)S(1)} collective-permute-done((f32[520,128]{1,0:T(8,128)S(1)}, f32[520,128]{1,0:T(8,128)S(1)}, u32[]{:S(2)}, u32[]{:S(2)}) %collective-permute-start.3) | collective-permute-done | bytes 266272 | tf_op jit(solution)/shard_map/spread/ppermute | solution.py:49
  44.6 2.3 %bands.1 = (bf16[128,256]{1,0:T(8,128)(2,1)S(1)}, bf16[128,256]{1,0:T(8,128)(2,1)S(1)}, bf16[4,256,256]{2,1,0:T(8,128)(2,1)S(1)}, bf16[4,256,256]{2,1,0:T(8,128)(2,1)S(1)}) custom-call(f32[4,8,128]{2,1,0:T(8,128)S(1)} %get-tuple-element.32.taps), custom_call_target="tpu_custom_call" | custom-call | flops 30000000 | bytes 16384 | tf_op jit(solution)/shard_map/bands/pallas_call | solution.py:108
  47.3 3.9 %forward.2.fwd = f32[4,16,32,128]{3,2,1,0:T(8,128)S(1)} custom-call(f32[4,8,128]{2,1,0:T(8,128)S(1)} %get-tuple-element.32.taps, f32[16,64,128]{2,1,0:T(8,128)S(1)} %collective-permute-done.5.before, f32[16,64,128]{2,1,0:T(8,128)S(1)} %collective-permute-done.4.own.ext, f32[16,64,128]{2,1,0:T(8,128)S(1)} %collective-permute-done.6.after, ...), custom_call_target="tpu_custom_call" | custom-call | flops 20000000000 | bytes 2179072 | tf_op jit(solution)/shard_map/forward/pallas_call | solution.py:108
  52.2 3.8 %collective-permute-done.7.lower = f32[1536,128]{1,0:T(8,128)S(1)} collective-permute-done((f32[1536,128]{1,0:T(8,128)S(1)}, f32[1536,128]{1,0:T(8,128)S(1)}, u32[]{:S(2)}, u32[]{:S(2)}) %collective-permute-start.7) | collective-permute-done | bytes 786464 | tf_op jit(solution)/shard_map/shift/ppermute | solution.py:63
  56.0 5.5 %back.2 = (f32[15,64,128]{2,1,0:T(8,128)S(1)}, f32[16,64,128]{2,1,0:T(8,128)S(1)}, f32[15,64,128]{2,1,0:T(8,128)S(1)}, f32[4,16,32,128]{3,2,1,0:T(8,128)S(1)}) custom-call(f32[4,8,128]{2,1,0:T(8,128)S(1)} %get-tuple-element.32.taps, f32[4,16,32,128]{3,2,1,0:T(8,128)} %copy-done.6, f32[520,128]{1,0:T(8,128)S(1)} %collective-permute-done.a0, ...), custom_call_target="tpu_custom_call" | custom-call | flops 2000000000 | bytes 4292608 | tf_op jit(solution)/shard_map/back/pallas_call | solution.py:108
  63.1 6.5 %collective-permute-done.9.from_prev = f32[15,64,128]{2,1,0:T(8,128)S(1)} collective-permute-done((f32[15,64,128]{2,1,0:T(8,128)S(1)}, f32[15,64,128]{2,1,0:T(8,128)S(1)}, u32[]{:S(2)}, u32[]{:S(2)}) %collective-permute-start.9) | collective-permute-done | bytes 491552 | tf_op jit(solution)/shard_map/layers_out/ppermute | solution.py:63
  72.5 3.8 %collective-permute-done.12.from_next = f32[16,32,128]{2,1,0:T(8,128)S(1)} collective-permute-done((f32[16,32,128]{2,1,0:T(8,128)S(1)}, f32[16,32,128]{2,1,0:T(8,128)S(1)}, u32[]{:S(2)}, u32[]{:S(2)}) %collective-permute-start.12) | collective-permute-done | bytes 262176 | tf_op jit(solution)/shard_map/rows/ppermute | solution.py:68
  77.1 2.8 %collective-permute-start.14 = (f32[16,64,128]{2,1,0:T(8,128)S(1)}, f32[16,64,128]{2,1,0:T(8,128)S(1)}, u32[]{:S(2)}, u32[]{:S(2)}) collective-permute-start(f32[16,64,128]{2,1,0:T(8,128)S(1)} %rows.5.own.ext), channel_id=1, source_target_pairs={{0,194},{4,198},{8,202},{12,206},{1,0},{5,4},{9,8},{13,12},{17,1},... | collective-permute-start | bytes 1572872 | tf_op jit(solution)/shard_map/layers_in/ppermute | solution.py:63
  82.0 4.0 %collective-permute-done.14.after = f32[16,64,128]{2,1,0:T(8,128)S(1)} collective-permute-done((f32[16,64,128]{2,1,0:T(8,128)S(1)}, f32[16,64,128]{2,1,0:T(8,128)S(1)}, u32[]{:S(2)}, u32[]{:S(2)}) %collective-permute-start.14) | collective-permute-done | bytes 524320 | tf_op jit(solution)/shard_map/layers_in/ppermute | solution.py:63
  86.1 4.2 %collective-permute-done.13.before = f32[16,64,128]{2,1,0:T(8,128)S(1)} collective-permute-done((f32[16,64,128]{2,1,0:T(8,128)S(1)}, f32[16,64,128]{2,1,0:T(8,128)S(1)}, u32[]{:S(2)}, u32[]{:S(2)}) %collective-permute-start.13) | collective-permute-done | bytes 524320 | tf_op jit(solution)/shard_map/layers_in/ppermute | solution.py:63
  90.3 3.9 %forward.3.fwd = f32[4,16,32,128]{3,2,1,0:T(8,128)S(1)} custom-call(f32[4,8,128]{2,1,0:T(8,128)S(1)} %get-tuple-element.32.taps, f32[16,64,128]{2,1,0:T(8,128)S(1)} %collective-permute-done.13.before, f32[16,64,128]{2,1,0:T(8,128)S(1)} %rows.5.own.ext, f32[16,64,128]{2,1,0:T(8,128)S(1)} %collective-permute-done.14.after, ...), custom_call_target="tpu_custom_call" | custom-call | flops 2000000000 | bytes 2179072 | tf_op jit(solution)/shard_map/forward/pallas_call | solution.py:108
  94.2 3.8 %back.3 = (f32[15,64,128]{2,1,0:T(8,128)S(1)}, f32[16,64,128]{2,1,0:T(8,128)S(1)}, f32[15,64,128]{2,1,0:T(8,128)S(1)}) custom-call(f32[4,8,128]{2,1,0:T(8,128)S(1)} %get-tuple-element.32.taps, f32[4,16,32,128]{3,2,1,0:T(8,128)S(1)} %forward.3.fwd, f32[4,16,32,128]{3,2,1,0:T(8,128)S(1)} %get-tuple-element.44.rec, ...), custom_call_target="tpu_custom_call" | custom-call | flops 2000000000 | bytes 2703360 | tf_op jit(solution)/shard_map/back/pallas_call | solution.py:108
  99.5 6.5 %collective-permute-done.15.from_prev = f32[15,64,128]{2,1,0:T(8,128)S(1)} collective-permute-done((f32[15,64,128]{2,1,0:T(8,128)S(1)}, f32[15,64,128]{2,1,0:T(8,128)S(1)}, u32[]{:S(2)}, u32[]{:S(2)}) %collective-permute-start.15) | collective-permute-done | bytes 491552 | tf_op jit(solution)/shard_map/layers_out/ppermute | solution.py:63
  106.2 2.7 %collective-permute-start.17 = (f32[16,16,128]{2,1,0:T(8,128)S(1)}, f32[16,16,128]{2,1,0:T(8,128)S(1)}, u32[]{:S(2)}, u32[]{:S(2)}) collective-permute-start(f32[16,16,128]{2,1,0:T(8,128)S(1)} %get-tuple-element.49), channel_id=1, source_target_pairs={{0,4},{4,8},{8,12},{12,0},{1,5},{5,9},{9,13},{13,1},{17,21},{21,25... | collective-permute-start | bytes 393224 | tf_op jit(solution)/shard_map/rows/ppermute | solution.py:68
  110.8 3.1 %collective-permute-done.18.from_next = f32[16,16,128]{2,1,0:T(8,128)S(1)} collective-permute-done((f32[16,16,128]{2,1,0:T(8,128)S(1)}, f32[16,16,128]{2,1,0:T(8,128)S(1)}, u32[]{:S(2)}, u32[]{:S(2)}) %collective-permute-start.18) | collective-permute-done | bytes 131104 | tf_op jit(solution)/shard_map/rows/ppermute | solution.py:68
  114.8 8.4 %collective-permute-start.21 = (f32[16,32,128]{2,1,0:T(8,128)S(1)}, f32[16,32,128]{2,1,0:T(8,128)S(1)}, u32[]{:S(2)}, u32[]{:S(2)}) collective-permute-start(f32[16,32,128]{2,1,0:T(8,128)S(1)} %rows.7), channel_id=1, source_target_pairs={{0,0},{8,1},{4,2},{12,3},{5,4},{13,5},{9,6},{1,7},{25,8},{17,9},{2... | collective-permute-start | bytes 786440 | tf_op jit(solution)/shard_map/result/ppermute | solution.py:54
  125.1 19.2 %collective-permute-done.21.c2 = f32[16,32,128]{2,1,0:T(8,128)S(1)} collective-permute-done((f32[16,32,128]{2,1,0:T(8,128)S(1)}, f32[16,32,128]{2,1,0:T(8,128)S(1)}, u32[]{:S(2)}, u32[]{:S(2)}) %collective-permute-start.21) | collective-permute-done | bytes 262176 | tf_op jit(solution)/shard_map/result/ppermute | solution.py:54
  (49 shorter events, 27.1 us)
Async XLA Ops:
  1.2 4.9 %copy-start.5 = (f32[1,31]{1,0:T(1,128)S(1)}, f32[1,31]{1,0:T(1,128)}, u32[]{:S(2)}) copy-start(f32[1,31]{1,0:T(1,128)} %psf_x.1) | copy-start | bytes 376
  1.3 22.0 %collective-permute-start.4 = (f32[16,64,128]{2,1,0:T(8,128)S(1)}, f32[16,64,128]{2,1,0:T(8,128)S(1)}, u32[]{:S(2)}, u32[]{:S(2)}) collective-permute-start(f32[16,64,128]{2,1,0:T(8,128)S(1)} %window.1), channel_id=1, source_target_pairs={{0,4},{1,12},{2,0},{3,8},{4,9},{5,1},{6,5},{7,13},{8,29},{9,21},{1... | collective-permute-start | bytes 1572872 | tf_op jit(solution)/shard_map/window/ppermute | solution.py:49
  8.4 23.2 %collective-permute-start = (f32[520,128]{1,0:T(8,128)S(1)}, f32[520,128]{1,0:T(8,128)S(1)}, u32[]{:S(2)}, u32[]{:S(2)}) collective-permute-start(f32[520,128]{1,0:T(8,128)S(1)} %get-tuple-element.28), channel_id=1, source_target_pairs={{0,4},{1,12},{2,0},{3,8},{4,9},{5,1},{6,5},{7,13},{8,29},{9,21},{1... | collective-permute-start | bytes 798728 | tf_op jit(solution)/shard_map/spread/ppermute | solution.py:49
  10.8 20.7 %collective-permute-start.1 = (f32[520,128]{1,0:T(8,128)S(1)}, f32[520,128]{1,0:T(8,128)S(1)}, u32[]{:S(2)}, u32[]{:S(2)}) collective-permute-start(f32[520,128]{1,0:T(8,128)S(1)} %get-tuple-element.29), channel_id=1, source_target_pairs={{0,12},{1,4},{2,8},{3,0},{4,1},{5,9},{6,13},{7,5},{8,21},{9,29},{1... | collective-permute-start | bytes 798728 | tf_op jit(solution)/shard_map/spread/ppermute | solution.py:49
  13.4 23.3 %collective-permute-start.2 = (f32[520,128]{1,0:T(8,128)S(1)}, f32[520,128]{1,0:T(8,128)S(1)}, u32[]{:S(2)}, u32[]{:S(2)}) collective-permute-start(f32[520,128]{1,0:T(8,128)S(1)} %get-tuple-element.30), channel_id=1, source_target_pairs={{0,0},{1,8},{2,4},{3,12},{4,5},{5,13},{6,9},{7,1},{8,25},{9,17},{1... | collective-permute-start | bytes 798728 | tf_op jit(solution)/shard_map/spread/ppermute | solution.py:49
  20.9 20.2 %collective-permute-start.3 = (f32[520,128]{1,0:T(8,128)S(1)}, f32[520,128]{1,0:T(8,128)S(1)}, u32[]{:S(2)}, u32[]{:S(2)}) collective-permute-start(f32[520,128]{1,0:T(8,128)S(1)} %get-tuple-element.31), channel_id=1, source_target_pairs={{0,8},{1,0},{2,12},{3,4},{4,13},{5,5},{6,1},{7,9},{8,17},{9,25},{1... | collective-permute-start | bytes 798728 | tf_op jit(solution)/shard_map/spread/ppermute | solution.py:49
  23.3 23.6 %collective-permute-start.6 = (f32[16,64,128]{2,1,0:T(8,128)S(1)}, f32[16,64,128]{2,1,0:T(8,128)S(1)}, u32[]{:S(2)}, u32[]{:S(2)}) collective-permute-start(f32[16,64,128]{2,1,0:T(8,128)S(1)} %collective-permute-done.4.own.ext), channel_id=1, source_target_pairs={{0,194},{4,198},{8,202},{12,206},{1,0},{5,4},{9,8},{13,12},{17,1},... | collective-permute-start | bytes 1572872 | tf_op jit(solution)/shard_map/layers_in/ppermute | solution.py:63
  31.6 15.7 %collective-permute-start.5 = (f32[16,64,128]{2,1,0:T(8,128)S(1)}, f32[16,64,128]{2,1,0:T(8,128)S(1)}, u32[]{:S(2)}, u32[]{:S(2)}) collective-permute-start(f32[16,64,128]{2,1,0:T(8,128)S(1)} %collective-permute-done.4.own.ext), channel_id=1, source_target_pairs={{0,1},{4,5},{8,9},{12,13},{1,17},{5,21},{9,25},{13,29},{17,16},{21... | collective-permute-start | bytes 1572872 | tf_op jit(solution)/shard_map/layers_in/ppermute | solution.py:63
  43.1 13.0 %collective-permute-start.7 = (f32[1536,128]{1,0:T(8,128)S(1)}, f32[1536,128]{1,0:T(8,128)S(1)}, u32[]{:S(2)}, u32[]{:S(2)}) collective-permute-start(f32[1536,128]{1,0:T(8,128)S(1)} %get-tuple-element.35), channel_id=1, source_target_pairs={{0,1},{4,5},{8,9},{12,13},{1,17},{5,21},{9,25},{13,29},{17,16},{21... | collective-permute-start | bytes 2359304 | tf_op jit(solution)/shard_map/shift/ppermute | solution.py:63
  44.4 11.7 %collective-permute-start.8 = (f32[1536,128]{1,0:T(8,128)S(1)}, f32[1536,128]{1,0:T(8,128)S(1)}, u32[]{:S(2)}, u32[]{:S(2)}) collective-permute-start(f32[1536,128]{1,0:T(8,128)S(1)} %get-tuple-element.36), channel_id=1, source_target_pairs={{0,194},{4,198},{8,202},{12,206},{1,0},{5,4},{9,8},{13,12},{17,1},... | collective-permute-start | bytes 2359304 | tf_op jit(solution)/shard_map/shift/ppermute | solution.py:63
  61.5 8.1 %collective-permute-start.9 = (f32[15,64,128]{2,1,0:T(8,128)S(1)}, f32[15,64,128]{2,1,0:T(8,128)S(1)}, u32[]{:S(2)}, u32[]{:S(2)}) collective-permute-start(f32[15,64,128]{2,1,0:T(8,128)S(1)} %get-tuple-element.40), channel_id=1, source_target_pairs={{0,1},{4,5},{8,9},{12,13},{1,17},{5,21},{9,25},{13,29},{17,16},{21... | collective-permute-start | bytes 1474568 | tf_op jit(solution)/shard_map/layers_out/ppermute | solution.py:63
  62.9 6.7 %collective-permute-start.10 = (f32[15,64,128]{2,1,0:T(8,128)S(1)}, f32[15,64,128]{2,1,0:T(8,128)S(1)}, u32[]{:S(2)}, u32[]{:S(2)}) collective-permute-start(f32[15,64,128]{2,1,0:T(8,128)S(1)} %get-tuple-element.41), channel_id=1, source_target_pairs={{0,194},{4,198},{8,202},{12,206},{1,0},{5,4},{9,8},{13,12},{17,1},... | collective-permute-start | bytes 1474568 | tf_op jit(solution)/shard_map/layers_out/ppermute | solution.py:63
  69.7 6.5 %collective-permute-start.12 = (f32[16,32,128]{2,1,0:T(8,128)S(1)}, f32[16,32,128]{2,1,0:T(8,128)S(1)}, u32[]{:S(2)}, u32[]{:S(2)}) collective-permute-start(f32[16,32,128]{2,1,0:T(8,128)S(1)} %get-tuple-element.42.low), channel_id=1, source_target_pairs={{0,12},{4,0},{8,4},{12,8},{1,13},{5,1},{9,5},{13,9},{17,29},{21,17... | collective-permute-start | bytes 786440 | tf_op jit(solution)/shard_map/rows/ppermute | solution.py:68
  70.9 5.3 %collective-permute-start.11 = (f32[16,32,128]{2,1,0:T(8,128)S(1)}, f32[16,32,128]{2,1,0:T(8,128)S(1)}, u32[]{:S(2)}, u32[]{:S(2)}) collective-permute-start(f32[16,32,128]{2,1,0:T(8,128)S(1)} %get-tuple-element.43.high), channel_id=1, source_target_pairs={{0,4},{4,8},{8,12},{12,0},{1,5},{5,9},{9,13},{13,1},{17,21},{21,25... | collective-permute-start | bytes 786440 | tf_op jit(solution)/shard_map/rows/ppermute | solution.py:68
  77.1 8.9 %collective-permute-start.14 = (f32[16,64,128]{2,1,0:T(8,128)S(1)}, f32[16,64,128]{2,1,0:T(8,128)S(1)}, u32[]{:S(2)}, u32[]{:S(2)}) collective-permute-start(f32[16,64,128]{2,1,0:T(8,128)S(1)} %rows.5.own.ext), channel_id=1, source_target_pairs={{0,194},{4,198},{8,202},{12,206},{1,0},{5,4},{9,8},{13,12},{17,1},... | collective-permute-start | bytes 1572872 | tf_op jit(solution)/shard_map/layers_in/ppermute | solution.py:63
  79.9 10.3 %collective-permute-start.13 = (f32[16,64,128]{2,1,0:T(8,128)S(1)}, f32[16,64,128]{2,1,0:T(8,128)S(1)}, u32[]{:S(2)}, u32[]{:S(2)}) collective-permute-start(f32[16,64,128]{2,1,0:T(8,128)S(1)} %rows.5.own.ext), channel_id=1, source_target_pairs={{0,1},{4,5},{8,9},{12,13},{1,17},{5,21},{9,25},{13,29},{17,16},{21... | collective-permute-start | bytes 1572872 | tf_op jit(solution)/shard_map/layers_in/ppermute | solution.py:63
  98.0 8.1 %collective-permute-start.15 = (f32[15,64,128]{2,1,0:T(8,128)S(1)}, f32[15,64,128]{2,1,0:T(8,128)S(1)}, u32[]{:S(2)}, u32[]{:S(2)}) collective-permute-start(f32[15,64,128]{2,1,0:T(8,128)S(1)} %get-tuple-element.46), channel_id=1, source_target_pairs={{0,1},{4,5},{8,9},{12,13},{1,17},{5,21},{9,25},{13,29},{17,16},{21... | collective-permute-start | bytes 1474568 | tf_op jit(solution)/shard_map/layers_out/ppermute | solution.py:63
  99.5 6.5 %collective-permute-start.16 = (f32[15,64,128]{2,1,0:T(8,128)S(1)}, f32[15,64,128]{2,1,0:T(8,128)S(1)}, u32[]{:S(2)}, u32[]{:S(2)}) collective-permute-start(f32[15,64,128]{2,1,0:T(8,128)S(1)} %get-tuple-element.47), channel_id=1, source_target_pairs={{0,194},{4,198},{8,202},{12,206},{1,0},{5,4},{9,8},{13,12},{17,1},... | collective-permute-start | bytes 1474568 | tf_op jit(solution)/shard_map/layers_out/ppermute | solution.py:63
  106.2 4.7 %collective-permute-start.17 = (f32[16,16,128]{2,1,0:T(8,128)S(1)}, f32[16,16,128]{2,1,0:T(8,128)S(1)}, u32[]{:S(2)}, u32[]{:S(2)}) collective-permute-start(f32[16,16,128]{2,1,0:T(8,128)S(1)} %get-tuple-element.49), channel_id=1, source_target_pairs={{0,4},{4,8},{8,12},{12,0},{1,5},{5,9},{9,13},{13,1},{17,21},{21,25... | collective-permute-start | bytes 393224 | tf_op jit(solution)/shard_map/rows/ppermute | solution.py:68
  108.9 5.0 %collective-permute-start.18 = (f32[16,16,128]{2,1,0:T(8,128)S(1)}, f32[16,16,128]{2,1,0:T(8,128)S(1)}, u32[]{:S(2)}, u32[]{:S(2)}) collective-permute-start(f32[16,16,128]{2,1,0:T(8,128)S(1)} %get-tuple-element.50), channel_id=1, source_target_pairs={{0,12},{4,0},{8,4},{12,8},{1,13},{5,1},{9,5},{13,9},{17,29},{21,17... | collective-permute-start | bytes 393224 | tf_op jit(solution)/shard_map/rows/ppermute | solution.py:68
  114.8 29.5 %collective-permute-start.21 = (f32[16,32,128]{2,1,0:T(8,128)S(1)}, f32[16,32,128]{2,1,0:T(8,128)S(1)}, u32[]{:S(2)}, u32[]{:S(2)}) collective-permute-start(f32[16,32,128]{2,1,0:T(8,128)S(1)} %rows.7), channel_id=1, source_target_pairs={{0,0},{8,1},{4,2},{12,3},{5,4},{13,5},{9,6},{1,7},{25,8},{17,9},{2... | collective-permute-start | bytes 786440 | tf_op jit(solution)/shard_map/result/ppermute | solution.py:54
  123.2 22.8 %collective-permute-start.19 = (f32[16,32,128]{2,1,0:T(8,128)S(1)}, f32[16,32,128]{2,1,0:T(8,128)S(1)}, u32[]{:S(2)}, u32[]{:S(2)}) collective-permute-start(f32[16,32,128]{2,1,0:T(8,128)S(1)} %rows.7), channel_id=1, source_target_pairs={{4,0},{12,1},{0,2},{8,3},{9,4},{1,5},{5,6},{13,7},{29,8},{21,9},{2... | collective-permute-start | bytes 786440 | tf_op jit(solution)/shard_map/result/ppermute | solution.py:54
  144.3 2.6 %collective-permute-start.22 = (f32[16,32,128]{2,1,0:T(8,128)S(1)}, f32[16,32,128]{2,1,0:T(8,128)S(1)}, u32[]{:S(2)}, u32[]{:S(2)}) collective-permute-start(f32[16,32,128]{2,1,0:T(8,128)S(1)} %collective-permute-done.21.c2), channel_id=1, source_target_pairs={{0,1},{1,0},{2,3},{3,2},{4,5},{5,4},{6,7},{7,6},{8,9},{9,8},{10,11... | collective-permute-start | bytes 786440 | tf_op jit(solution)/shard_map/result/ppermute | solution.py:58
  146.0 2.2 %collective-permute-start.20 = (f32[16,32,128]{2,1,0:T(8,128)S(1)}, f32[16,32,128]{2,1,0:T(8,128)S(1)}, u32[]{:S(2)}, u32[]{:S(2)}) collective-permute-start(f32[16,32,128]{2,1,0:T(8,128)S(1)} %collective-permute-done.19.c0), channel_id=1, source_target_pairs={{0,1},{1,0},{2,3},{3,2},{4,5},{5,4},{6,7},{7,6},{8,9},{9,8},{10,11... | collective-permute-start | bytes 786440 | tf_op jit(solution)/shard_map/result/ppermute | solution.py:58
  (6 other events, 21.7 us)

commit v3 on v2

--- a/solution.py
+++ b/solution.py
@@ -157,7 +157,7 @@
     back_y = lax.rem(LANES - dy, LANES)
     back_x = lax.rem(LANES - dx, LANES)
 
-    @pl.loop(0, BZ)
+    @pl.loop(0, BZ, unroll=4)
     def _(z):
         plane = pltpu.roll(pltpu.roll(rec[0, z], back_y, 0), back_x, 1)
         moved[z] = jnp.where(inside, plane, 0.0)
@@ -339,7 +339,7 @@
     for v in range(VIEWS):
         dz = shift_of(taps, v)
 
-        @pl.loop(0, BZ)
+        @pl.loop(0, BZ, unroll=8)
         def _(i, v=v, dz=dz, n_up=n_up, n_down=n_down):
             src = i + dz
             place_z = block * BZ + src

time: 150 us -> 149 us (level)
  transfers between devices with their start and end apart: 23 -> 23, of which waited for: 15 -> 15; matrix products, arithmetic and copies ran while one was open for 0% -> 0% of each run, Pallas kernels for 7% -> 6%
where the time goes in v3:
time: 149 us
  waiting for transfers between devices  74.5 us (50%)
  starting transfers between devices  46 us (31%)
  Pallas kernels  25.3 us (17%)
  local copies, waits for them, and re-layouts  2.24 us (2%)
    ppermute x10, waiting for transfers between devices, to_layer(): return lax.ppermute(x, AXES, perm)  25.8 us
    pallas_call x13, Pallas kernels, call(): pl.pallas_call(body, out_shape=outs, in_specs=specs, out_specs=out_specs...  25.3 us
    ppermute x2, waiting for transfers between devices, collect(): return lax.ppermute(x, AXES, perm)  20.1 us
    ppermute x5, starting transfers between devices, spread(): return lax.ppermute(x, AXES, perm)  19.1 us
    ppermute x5, waiting for transfers between devices, spread(): return lax.ppermute(x, AXES, perm)  18.6 us
    ppermute x2, starting transfers between devices, collect(): return lax.ppermute(x, AXES, perm)  10.3 us
    ppermute x10, starting transfers between devices, to_layer(): return lax.ppermute(x, AXES, perm)  9.66 us
    ppermute x4, waiting for transfers between devices, to_row(): return lax.ppermute(x, AXES, perm)  8.78 us
  transfers between devices with their start and end apart: 23, of which 15 were waited for; matrix products, arithmetic and copies ran while one was open for 0% of the time, Pallas kernels for 6%

profile of v3, /device:TPU:95, one launch (start us, length us, event | category | flops | bytes accessed | tf_op | source)
XLA Modules:
  0.0 148.9 jit_solution(12743929438226566863)
XLA Ops:
  1.3 4.2 %collective-permute-start.4 = (f32[16,64,128]{2,1,0:T(8,128)S(1)}, f32[16,64,128]{2,1,0:T(8,128)S(1)}, u32[]{:S(2)}, u32[]{:S(2)}) collective-permute-start(f32[16,64,128]{2,1,0:T(8,128)S(1)} %window.1), channel_id=1, source_target_pairs={{0,4},{1,12},{2,0},{3,8},{4,9},{5,1},{6,5},{7,13},{8,29},{9,21},{1... | collective-permute-start | bytes 1572872 | tf_op jit(solution)/shard_map/window/ppermute | solution.py:49
  7.4 2.5 %collective-permute-start = (f32[520,128]{1,0:T(8,128)S(1)}, f32[520,128]{1,0:T(8,128)S(1)}, u32[]{:S(2)}, u32[]{:S(2)}) collective-permute-start(f32[520,128]{1,0:T(8,128)S(1)} %get-tuple-element.28), channel_id=1, source_target_pairs={{0,4},{1,12},{2,0},{3,8},{4,9},{5,1},{6,5},{7,13},{8,29},{9,21},{1... | collective-permute-start | bytes 798728 | tf_op jit(solution)/shard_map/spread/ppermute | solution.py:49
  9.9 2.6 %collective-permute-start.1 = (f32[520,128]{1,0:T(8,128)S(1)}, f32[520,128]{1,0:T(8,128)S(1)}, u32[]{:S(2)}, u32[]{:S(2)}) collective-permute-start(f32[520,128]{1,0:T(8,128)S(1)} %get-tuple-element.29), channel_id=1, source_target_pairs={{0,12},{1,4},{2,8},{3,0},{4,1},{5,9},{6,13},{7,5},{8,21},{9,29},{1... | collective-permute-start | bytes 798728 | tf_op jit(solution)/shard_map/spread/ppermute | solution.py:49
  12.5 7.5 %collective-permute-start.2 = (f32[520,128]{1,0:T(8,128)S(1)}, f32[520,128]{1,0:T(8,128)S(1)}, u32[]{:S(2)}, u32[]{:S(2)}) collective-permute-start(f32[520,128]{1,0:T(8,128)S(1)} %get-tuple-element.30), channel_id=1, source_target_pairs={{0,0},{1,8},{2,4},{3,12},{4,5},{5,13},{6,9},{7,1},{8,25},{9,17},{1... | collective-permute-start | bytes 798728 | tf_op jit(solution)/shard_map/spread/ppermute | solution.py:49
  20.0 2.4 %collective-permute-start.3 = (f32[520,128]{1,0:T(8,128)S(1)}, f32[520,128]{1,0:T(8,128)S(1)}, u32[]{:S(2)}, u32[]{:S(2)}) collective-permute-start(f32[520,128]{1,0:T(8,128)S(1)} %get-tuple-element.31), channel_id=1, source_target_pairs={{0,8},{1,0},{2,12},{3,4},{4,13},{5,5},{6,1},{7,9},{8,17},{9,25},{1... | collective-permute-start | bytes 798728 | tf_op jit(solution)/shard_map/spread/ppermute | solution.py:49
  22.5 10.0 %collective-permute-done.a0 = f32[520,128]{1,0:T(8,128)S(1)} collective-permute-done((f32[520,128]{1,0:T(8,128)S(1)}, f32[520,128]{1,0:T(8,128)S(1)}, u32[]{:S(2)}, u32[]{:S(2)}) %collective-permute-start) | collective-permute-done | bytes 266272 | tf_op jit(solution)/shard_map/spread/ppermute | solution.py:49
  32.5 4.2 %collective-permute-done.2.a2 = f32[520,128]{1,0:T(8,128)S(1)} collective-permute-done((f32[520,128]{1,0:T(8,128)S(1)}, f32[520,128]{1,0:T(8,128)S(1)}, u32[]{:S(2)}, u32[]{:S(2)}) %collective-permute-start.2) | collective-permute-done | bytes 266272 | tf_op jit(solution)/shard_map/spread/ppermute | solution.py:49
  36.7 4.5 %collective-permute-done.3.a3 = f32[520,128]{1,0:T(8,128)S(1)} collective-permute-done((f32[520,128]{1,0:T(8,128)S(1)}, f32[520,128]{1,0:T(8,128)S(1)}, u32[]{:S(2)}, u32[]{:S(2)}) %collective-permute-start.3) | collective-permute-done | bytes 266272 | tf_op jit(solution)/shard_map/spread/ppermute | solution.py:49
  47.3 3.9 %forward.2.fwd = f32[4,16,32,128]{3,2,1,0:T(8,128)S(1)} custom-call(f32[4,8,128]{2,1,0:T(8,128)S(1)} %get-tuple-element.32.taps, f32[16,64,128]{2,1,0:T(8,128)S(1)} %collective-permute-done.5.before, f32[16,64,128]{2,1,0:T(8,128)S(1)} %collective-permute-done.4.own.ext, f32[16,64,128]{2,1,0:T(8,128)S(1)} %collective-permute-done.6.after, ...), custom_call_target="tpu_custom_call" | custom-call | flops 20000000000 | bytes 2179072 | tf_op jit(solution)/shard_map/forward/pallas_call | solution.py:108
  52.2 3.8 %collective-permute-done.7.lower = f32[1536,128]{1,0:T(8,128)S(1)} collective-permute-done((f32[1536,128]{1,0:T(8,128)S(1)}, f32[1536,128]{1,0:T(8,128)S(1)}, u32[]{:S(2)}, u32[]{:S(2)}) %collective-permute-start.7) | collective-permute-done | bytes 786464 | tf_op jit(solution)/shard_map/shift/ppermute | solution.py:63
  56.0 5.1 %back.2 = (f32[15,64,128]{2,1,0:T(8,128)S(1)}, f32[16,64,128]{2,1,0:T(8,128)S(1)}, f32[15,64,128]{2,1,0:T(8,128)S(1)}, f32[4,16,32,128]{3,2,1,0:T(8,128)S(1)}) custom-call(f32[4,8,128]{2,1,0:T(8,128)S(1)} %get-tuple-element.32.taps, f32[4,16,32,128]{3,2,1,0:T(8,128)} %copy-done.6, f32[520,128]{1,0:T(8,128)S(1)} %collective-permute-done.a0, ...), custom_call_target="tpu_custom_call" | custom-call | flops 2000000000 | bytes 4292608 | tf_op jit(solution)/shard_map/back/pallas_call | solution.py:108
  62.7 6.5 %collective-permute-done.9.from_prev = f32[15,64,128]{2,1,0:T(8,128)S(1)} collective-permute-done((f32[15,64,128]{2,1,0:T(8,128)S(1)}, f32[15,64,128]{2,1,0:T(8,128)S(1)}, u32[]{:S(2)}, u32[]{:S(2)}) %collective-permute-start.9) | collective-permute-done | bytes 491552 | tf_op jit(solution)/shard_map/layers_out/ppermute | solution.py:63
  72.1 3.8 %collective-permute-done.12.from_next = f32[16,32,128]{2,1,0:T(8,128)S(1)} collective-permute-done((f32[16,32,128]{2,1,0:T(8,128)S(1)}, f32[16,32,128]{2,1,0:T(8,128)S(1)}, u32[]{:S(2)}, u32[]{:S(2)}) %collective-permute-start.12) | collective-permute-done | bytes 262176 | tf_op jit(solution)/shard_map/rows/ppermute | solution.py:68
  76.8 2.5 %collective-permute-start.14 = (f32[16,64,128]{2,1,0:T(8,128)S(1)}, f32[16,64,128]{2,1,0:T(8,128)S(1)}, u32[]{:S(2)}, u32[]{:S(2)}) collective-permute-start(f32[16,64,128]{2,1,0:T(8,128)S(1)} %rows.5.own.ext), channel_id=1, source_target_pairs={{0,194},{4,198},{8,202},{12,206},{1,0},{5,4},{9,8},{13,12},{17,1},... | collective-permute-start | bytes 1572872 | tf_op jit(solution)/shard_map/layers_in/ppermute | solution.py:63
  79.2 2.4 %collective-permute-start.13 = (f32[16,64,128]{2,1,0:T(8,128)S(1)}, f32[16,64,128]{2,1,0:T(8,128)S(1)}, u32[]{:S(2)}, u32[]{:S(2)}) collective-permute-start(f32[16,64,128]{2,1,0:T(8,128)S(1)} %rows.5.own.ext), channel_id=1, source_target_pairs={{0,1},{4,5},{8,9},{12,13},{1,17},{5,21},{9,25},{13,29},{17,16},{21... | collective-permute-start | bytes 1572872 | tf_op jit(solution)/shard_map/layers_in/ppermute | solution.py:63
  81.7 3.7 %collective-permute-done.14.after = f32[16,64,128]{2,1,0:T(8,128)S(1)} collective-permute-done((f32[16,64,128]{2,1,0:T(8,128)S(1)}, f32[16,64,128]{2,1,0:T(8,128)S(1)}, u32[]{:S(2)}, u32[]{:S(2)}) %collective-permute-start.14) | collective-permute-done | bytes 524320 | tf_op jit(solution)/shard_map/layers_in/ppermute | solution.py:63
  85.4 4.9 %collective-permute-done.13.before = f32[16,64,128]{2,1,0:T(8,128)S(1)} collective-permute-done((f32[16,64,128]{2,1,0:T(8,128)S(1)}, f32[16,64,128]{2,1,0:T(8,128)S(1)}, u32[]{:S(2)}, u32[]{:S(2)}) %collective-permute-start.13) | collective-permute-done | bytes 524320 | tf_op jit(solution)/shard_map/layers_in/ppermute | solution.py:63
  90.3 3.9 %forward.3.fwd = f32[4,16,32,128]{3,2,1,0:T(8,128)S(1)} custom-call(f32[4,8,128]{2,1,0:T(8,128)S(1)} %get-tuple-element.32.taps, f32[16,64,128]{2,1,0:T(8,128)S(1)} %collective-permute-done.13.before, f32[16,64,128]{2,1,0:T(8,128)S(1)} %rows.5.own.ext, f32[16,64,128]{2,1,0:T(8,128)S(1)} %collective-permute-done.14.after, ...), custom_call_target="tpu_custom_call" | custom-call | flops 2000000000 | bytes 2179072 | tf_op jit(solution)/shard_map/forward/pallas_call | solution.py:108
  94.2 3.8 %back.3 = (f32[15,64,128]{2,1,0:T(8,128)S(1)}, f32[16,64,128]{2,1,0:T(8,128)S(1)}, f32[15,64,128]{2,1,0:T(8,128)S(1)}) custom-call(f32[4,8,128]{2,1,0:T(8,128)S(1)} %get-tuple-element.32.taps, f32[4,16,32,128]{3,2,1,0:T(8,128)S(1)} %forward.3.fwd, f32[4,16,32,128]{3,2,1,0:T(8,128)S(1)} %get-tuple-element.44.rec, ...), custom_call_target="tpu_custom_call" | custom-call | flops 2000000000 | bytes 2703360 | tf_op jit(solution)/shard_map/back/pallas_call | solution.py:108
  99.6 6.5 %collective-permute-done.15.from_prev = f32[15,64,128]{2,1,0:T(8,128)S(1)} collective-permute-done((f32[15,64,128]{2,1,0:T(8,128)S(1)}, f32[15,64,128]{2,1,0:T(8,128)S(1)}, u32[]{:S(2)}, u32[]{:S(2)}) %collective-permute-start.15) | collective-permute-done | bytes 491552 | tf_op jit(solution)/shard_map/layers_out/ppermute | solution.py:63
  106.2 2.7 %collective-permute-start.17 = (f32[16,16,128]{2,1,0:T(8,128)S(1)}, f32[16,16,128]{2,1,0:T(8,128)S(1)}, u32[]{:S(2)}, u32[]{:S(2)}) collective-permute-start(f32[16,16,128]{2,1,0:T(8,128)S(1)} %get-tuple-element.49), channel_id=1, source_target_pairs={{0,4},{4,8},{8,12},{12,0},{1,5},{5,9},{9,13},{13,1},{17,21},{21,25... | collective-permute-start | bytes 393224 | tf_op jit(solution)/shard_map/rows/ppermute | solution.py:68
  110.9 3.1 %collective-permute-done.18.from_next = f32[16,16,128]{2,1,0:T(8,128)S(1)} collective-permute-done((f32[16,16,128]{2,1,0:T(8,128)S(1)}, f32[16,16,128]{2,1,0:T(8,128)S(1)}, u32[]{:S(2)}, u32[]{:S(2)}) %collective-permute-start.18) | collective-permute-done | bytes 131104 | tf_op jit(solution)/shard_map/rows/ppermute | solution.py:68
  114.8 8.4 %collective-permute-start.21 = (f32[16,32,128]{2,1,0:T(8,128)S(1)}, f32[16,32,128]{2,1,0:T(8,128)S(1)}, u32[]{:S(2)}, u32[]{:S(2)}) collective-permute-start(f32[16,32,128]{2,1,0:T(8,128)S(1)} %rows.7), channel_id=1, source_target_pairs={{0,0},{8,1},{4,2},{12,3},{5,4},{13,5},{9,6},{1,7},{25,8},{17,9},{2... | collective-permute-start | bytes 786440 | tf_op jit(solution)/shard_map/result/ppermute | solution.py:54
  125.1 18.9 %collective-permute-done.21.c2 = f32[16,32,128]{2,1,0:T(8,128)S(1)} collective-permute-done((f32[16,32,128]{2,1,0:T(8,128)S(1)}, f32[16,32,128]{2,1,0:T(8,128)S(1)}, u32[]{:S(2)}, u32[]{:S(2)}) %collective-permute-start.21) | collective-permute-done | bytes 262176 | tf_op jit(solution)/shard_map/result/ppermute | solution.py:54
  (49 shorter events, 26.3 us)
Async XLA Ops:
  1.2 4.9 %copy-start.5 = (f32[1,31]{1,0:T(1,128)S(1)}, f32[1,31]{1,0:T(1,128)}, u32[]{:S(2)}) copy-start(f32[1,31]{1,0:T(1,128)} %psf_x.1) | copy-start | bytes 376
  1.3 21.1 %collective-permute-start.4 = (f32[16,64,128]{2,1,0:T(8,128)S(1)}, f32[16,64,128]{2,1,0:T(8,128)S(1)}, u32[]{:S(2)}, u32[]{:S(2)}) collective-permute-start(f32[16,64,128]{2,1,0:T(8,128)S(1)} %window.1), channel_id=1, source_target_pairs={{0,4},{1,12},{2,0},{3,8},{4,9},{5,1},{6,5},{7,13},{8,29},{9,21},{1... | collective-permute-start | bytes 1572872 | tf_op jit(solution)/shard_map/window/ppermute | solution.py:49
  7.4 25.0 %collective-permute-start = (f32[520,128]{1,0:T(8,128)S(1)}, f32[520,128]{1,0:T(8,128)S(1)}, u32[]{:S(2)}, u32[]{:S(2)}) collective-permute-start(f32[520,128]{1,0:T(8,128)S(1)} %get-tuple-element.28), channel_id=1, source_target_pairs={{0,4},{1,12},{2,0},{3,8},{4,9},{5,1},{6,5},{7,13},{8,29},{9,21},{1... | collective-permute-start | bytes 798728 | tf_op jit(solution)/shard_map/spread/ppermute | solution.py:49
  9.9 22.6 %collective-permute-start.1 = (f32[520,128]{1,0:T(8,128)S(1)}, f32[520,128]{1,0:T(8,128)S(1)}, u32[]{:S(2)}, u32[]{:S(2)}) collective-permute-start(f32[520,128]{1,0:T(8,128)S(1)} %get-tuple-element.29), channel_id=1, source_target_pairs={{0,12},{1,4},{2,8},{3,0},{4,1},{5,9},{6,13},{7,5},{8,21},{9,29},{1... | collective-permute-start | bytes 798728 | tf_op jit(solution)/shard_map/spread/ppermute | solution.py:49
  12.5 24.2 %collective-permute-start.2 = (f32[520,128]{1,0:T(8,128)S(1)}, f32[520,128]{1,0:T(8,128)S(1)}, u32[]{:S(2)}, u32[]{:S(2)}) collective-permute-start(f32[520,128]{1,0:T(8,128)S(1)} %get-tuple-element.30), channel_id=1, source_target_pairs={{0,0},{1,8},{2,4},{3,12},{4,5},{5,13},{6,9},{7,1},{8,25},{9,17},{1... | collective-permute-start | bytes 798728 | tf_op jit(solution)/shard_map/spread/ppermute | solution.py:49
  20.0 21.1 %collective-permute-start.3 = (f32[520,128]{1,0:T(8,128)S(1)}, f32[520,128]{1,0:T(8,128)S(1)}, u32[]{:S(2)}, u32[]{:S(2)}) collective-permute-start(f32[520,128]{1,0:T(8,128)S(1)} %get-tuple-element.31), channel_id=1, source_target_pairs={{0,8},{1,0},{2,12},{3,4},{4,13},{5,5},{6,1},{7,9},{8,17},{9,25},{1... | collective-permute-start | bytes 798728 | tf_op jit(solution)/shard_map/spread/ppermute | solution.py:49
  22.4 24.5 %collective-permute-start.6 = (f32[16,64,128]{2,1,0:T(8,128)S(1)}, f32[16,64,128]{2,1,0:T(8,128)S(1)}, u32[]{:S(2)}, u32[]{:S(2)}) collective-permute-start(f32[16,64,128]{2,1,0:T(8,128)S(1)} %collective-permute-done.4.own.ext), channel_id=1, source_target_pairs={{0,194},{4,198},{8,202},{12,206},{1,0},{5,4},{9,8},{13,12},{17,1},... | collective-permute-start | bytes 1572872 | tf_op jit(solution)/shard_map/layers_in/ppermute | solution.py:63
  32.5 14.8 %collective-permute-start.5 = (f32[16,64,128]{2,1,0:T(8,128)S(1)}, f32[16,64,128]{2,1,0:T(8,128)S(1)}, u32[]{:S(2)}, u32[]{:S(2)}) collective-permute-start(f32[16,64,128]{2,1,0:T(8,128)S(1)} %collective-permute-done.4.own.ext), channel_id=1, source_target_pairs={{0,1},{4,5},{8,9},{12,13},{1,17},{5,21},{9,25},{13,29},{17,16},{21... | collective-permute-start | bytes 1572872 | tf_op jit(solution)/shard_map/layers_in/ppermute | solution.py:63
  43.1 13.0 %collective-permute-start.7 = (f32[1536,128]{1,0:T(8,128)S(1)}, f32[1536,128]{1,0:T(8,128)S(1)}, u32[]{:S(2)}, u32[]{:S(2)}) collective-permute-start(f32[1536,128]{1,0:T(8,128)S(1)} %get-tuple-element.35), channel_id=1, source_target_pairs={{0,1},{4,5},{8,9},{12,13},{1,17},{5,21},{9,25},{13,29},{17,16},{21... | collective-permute-start | bytes 2359304 | tf_op jit(solution)/shard_map/shift/ppermute | solution.py:63
  44.4 11.7 %collective-permute-start.8 = (f32[1536,128]{1,0:T(8,128)S(1)}, f32[1536,128]{1,0:T(8,128)S(1)}, u32[]{:S(2)}, u32[]{:S(2)}) collective-permute-start(f32[1536,128]{1,0:T(8,128)S(1)} %get-tuple-element.36), channel_id=1, source_target_pairs={{0,194},{4,198},{8,202},{12,206},{1,0},{5,4},{9,8},{13,12},{17,1},... | collective-permute-start | bytes 2359304 | tf_op jit(solution)/shard_map/shift/ppermute | solution.py:63
  61.2 8.1 %collective-permute-start.9 = (f32[15,64,128]{2,1,0:T(8,128)S(1)}, f32[15,64,128]{2,1,0:T(8,128)S(1)}, u32[]{:S(2)}, u32[]{:S(2)}) collective-permute-start(f32[15,64,128]{2,1,0:T(8,128)S(1)} %get-tuple-element.40), channel_id=1, source_target_pairs={{0,1},{4,5},{8,9},{12,13},{1,17},{5,21},{9,25},{13,29},{17,16},{21... | collective-permute-start | bytes 1474568 | tf_op jit(solution)/shard_map/layers_out/ppermute | solution.py:63
  62.6 6.7 %collective-permute-start.10 = (f32[15,64,128]{2,1,0:T(8,128)S(1)}, f32[15,64,128]{2,1,0:T(8,128)S(1)}, u32[]{:S(2)}, u32[]{:S(2)}) collective-permute-start(f32[15,64,128]{2,1,0:T(8,128)S(1)} %get-tuple-element.41), channel_id=1, source_target_pairs={{0,194},{4,198},{8,202},{12,206},{1,0},{5,4},{9,8},{13,12},{17,1},... | collective-permute-start | bytes 1474568 | tf_op jit(solution)/shard_map/layers_out/ppermute | solution.py:63
  69.4 6.5 %collective-permute-start.12 = (f32[16,32,128]{2,1,0:T(8,128)S(1)}, f32[16,32,128]{2,1,0:T(8,128)S(1)}, u32[]{:S(2)}, u32[]{:S(2)}) collective-permute-start(f32[16,32,128]{2,1,0:T(8,128)S(1)} %get-tuple-element.42.low), channel_id=1, source_target_pairs={{0,12},{4,0},{8,4},{12,8},{1,13},{5,1},{9,5},{13,9},{17,29},{21,17... | collective-permute-start | bytes 786440 | tf_op jit(solution)/shard_map/rows/ppermute | solution.py:68
  70.6 5.3 %collective-permute-start.11 = (f32[16,32,128]{2,1,0:T(8,128)S(1)}, f32[16,32,128]{2,1,0:T(8,128)S(1)}, u32[]{:S(2)}, u32[]{:S(2)}) collective-permute-start(f32[16,32,128]{2,1,0:T(8,128)S(1)} %get-tuple-element.43.high), channel_id=1, source_target_pairs={{0,4},{4,8},{8,12},{12,0},{1,5},{5,9},{9,13},{13,1},{17,21},{21,25... | collective-permute-start | bytes 786440 | tf_op jit(solution)/shard_map/rows/ppermute | solution.py:68
  76.8 8.6 %collective-permute-start.14 = (f32[16,64,128]{2,1,0:T(8,128)S(1)}, f32[16,64,128]{2,1,0:T(8,128)S(1)}, u32[]{:S(2)}, u32[]{:S(2)}) collective-permute-start(f32[16,64,128]{2,1,0:T(8,128)S(1)} %rows.5.own.ext), channel_id=1, source_target_pairs={{0,194},{4,198},{8,202},{12,206},{1,0},{5,4},{9,8},{13,12},{17,1},... | collective-permute-start | bytes 1572872 | tf_op jit(solution)/shard_map/layers_in/ppermute | solution.py:63
  79.2 11.1 %collective-permute-start.13 = (f32[16,64,128]{2,1,0:T(8,128)S(1)}, f32[16,64,128]{2,1,0:T(8,128)S(1)}, u32[]{:S(2)}, u32[]{:S(2)}) collective-permute-start(f32[16,64,128]{2,1,0:T(8,128)S(1)} %rows.5.own.ext), channel_id=1, source_target_pairs={{0,1},{4,5},{8,9},{12,13},{1,17},{5,21},{9,25},{13,29},{17,16},{21... | collective-permute-start | bytes 1572872 | tf_op jit(solution)/shard_map/layers_in/ppermute | solution.py:63
  98.0 8.1 %collective-permute-start.15 = (f32[15,64,128]{2,1,0:T(8,128)S(1)}, f32[15,64,128]{2,1,0:T(8,128)S(1)}, u32[]{:S(2)}, u32[]{:S(2)}) collective-permute-start(f32[15,64,128]{2,1,0:T(8,128)S(1)} %get-tuple-element.46), channel_id=1, source_target_pairs={{0,1},{4,5},{8,9},{12,13},{1,17},{5,21},{9,25},{13,29},{17,16},{21... | collective-permute-start | bytes 1474568 | tf_op jit(solution)/shard_map/layers_out/ppermute | solution.py:63
  99.1 7.0 %collective-permute-start.16 = (f32[15,64,128]{2,1,0:T(8,128)S(1)}, f32[15,64,128]{2,1,0:T(8,128)S(1)}, u32[]{:S(2)}, u32[]{:S(2)}) collective-permute-start(f32[15,64,128]{2,1,0:T(8,128)S(1)} %get-tuple-element.47), channel_id=1, source_target_pairs={{0,194},{4,198},{8,202},{12,206},{1,0},{5,4},{9,8},{13,12},{17,1},... | collective-permute-start | bytes 1474568 | tf_op jit(solution)/shard_map/layers_out/ppermute | solution.py:63
  106.2 4.7 %collective-permute-start.17 = (f32[16,16,128]{2,1,0:T(8,128)S(1)}, f32[16,16,128]{2,1,0:T(8,128)S(1)}, u32[]{:S(2)}, u32[]{:S(2)}) collective-permute-start(f32[16,16,128]{2,1,0:T(8,128)S(1)} %get-tuple-element.49), channel_id=1, source_target_pairs={{0,4},{4,8},{8,12},{12,0},{1,5},{5,9},{9,13},{13,1},{17,21},{21,25... | collective-permute-start | bytes 393224 | tf_op jit(solution)/shard_map/rows/ppermute | solution.py:68
  108.9 5.0 %collective-permute-start.18 = (f32[16,16,128]{2,1,0:T(8,128)S(1)}, f32[16,16,128]{2,1,0:T(8,128)S(1)}, u32[]{:S(2)}, u32[]{:S(2)}) collective-permute-start(f32[16,16,128]{2,1,0:T(8,128)S(1)} %get-tuple-element.50), channel_id=1, source_target_pairs={{0,12},{4,0},{8,4},{12,8},{1,13},{5,1},{9,5},{13,9},{17,29},{21,17... | collective-permute-start | bytes 393224 | tf_op jit(solution)/shard_map/rows/ppermute | solution.py:68
  114.8 29.2 %collective-permute-start.21 = (f32[16,32,128]{2,1,0:T(8,128)S(1)}, f32[16,32,128]{2,1,0:T(8,128)S(1)}, u32[]{:S(2)}, u32[]{:S(2)}) collective-permute-start(f32[16,32,128]{2,1,0:T(8,128)S(1)} %rows.7), channel_id=1, source_target_pairs={{0,0},{8,1},{4,2},{12,3},{5,4},{13,5},{9,6},{1,7},{25,8},{17,9},{2... | collective-permute-start | bytes 786440 | tf_op jit(solution)/shard_map/result/ppermute | solution.py:54
  123.2 22.5 %collective-permute-start.19 = (f32[16,32,128]{2,1,0:T(8,128)S(1)}, f32[16,32,128]{2,1,0:T(8,128)S(1)}, u32[]{:S(2)}, u32[]{:S(2)}) collective-permute-start(f32[16,32,128]{2,1,0:T(8,128)S(1)} %rows.7), channel_id=1, source_target_pairs={{4,0},{12,1},{0,2},{8,3},{9,4},{1,5},{5,6},{13,7},{29,8},{21,9},{2... | collective-permute-start | bytes 786440 | tf_op jit(solution)/shard_map/result/ppermute | solution.py:54
  144.1 2.6 %collective-permute-start.22 = (f32[16,32,128]{2,1,0:T(8,128)S(1)}, f32[16,32,128]{2,1,0:T(8,128)S(1)}, u32[]{:S(2)}, u32[]{:S(2)}) collective-permute-start(f32[16,32,128]{2,1,0:T(8,128)S(1)} %collective-permute-done.21.c2), channel_id=1, source_target_pairs={{0,1},{1,0},{2,3},{3,2},{4,5},{5,4},{6,7},{7,6},{8,9},{9,8},{10,11... | collective-permute-start | bytes 786440 | tf_op jit(solution)/shard_map/result/ppermute | solution.py:58
  145.7 2.2 %collective-permute-start.20 = (f32[16,32,128]{2,1,0:T(8,128)S(1)}, f32[16,32,128]{2,1,0:T(8,128)S(1)}, u32[]{:S(2)}, u32[]{:S(2)}) collective-permute-start(f32[16,32,128]{2,1,0:T(8,128)S(1)} %collective-permute-done.19.c0), channel_id=1, source_target_pairs={{0,1},{1,0},{2,3},{3,2},{4,5},{5,4},{6,7},{7,6},{8,9},{9,8},{10,11... | collective-permute-start | bytes 786440 | tf_op jit(solution)/shard_map/result/ppermute | solution.py:58
  (6 other events, 21.7 us)

commit v4 on v3

--- a/solution.py
+++ b/solution.py
@@ -63,8 +63,9 @@
     return lax.ppermute(x, AXES, perm)
 
 
-def to_row(x, step):
-    perm = [(place(b, r), place(b, (r + step) % 4)) for b in range(64) for r in range(4)]
+def swap_row(x, j):
+    other = (1, 0, 3, 2) if j == 0 else (0, 2, 1, 3)
+    perm = [(place(b, r), place(b, other[r])) for b in range(64) for r in range(4)]
     return lax.ppermute(x, AXES, perm)
 
 
@@ -89,6 +90,10 @@
     _, r, block = position()
     far = lax.rem(r - lax.rem(block, 4) + 4, 4)
     return jnp.where(far == 1, 0, jnp.where(far == 3, 1, jnp.where(far == 0, 2, 3))) ^ j
+
+
+def by_parity(index, first, second):
+    return jnp.where((index & 1) == 0, first, second)
 
 
 def vmem():
@@ -371,40 +376,45 @@
     return out
 
 
-def halves_body(own, from_prev, from_next, low, high):
-    for out, cut in ((low, slice(0, ROWS)), (high, slice(ROWS, EXT))):
-        for i, value in enumerate(add_layers(own, from_prev, from_next, cut)):
-            out[i] = value
-
-
-def edges_body(own, from_prev, from_next, low, middle, high):
+def halves_body(own, from_prev, from_next, s0, s1):
+    _, r, _ = position()
+    low, high = (add_layers(own, from_prev, from_next, cut) for cut in (slice(0, ROWS), slice(ROWS, EXT)))
+    for i in range(BZ):
+        s0[i] = by_parity(r, high[i], low[i])
+        s1[i] = by_parity(r, low[i], high[i])
+
+
+def edges_body(own, from_prev, from_next, s0, middle, s1):
+    _, r, _ = position()
     cuts = (slice(0, EDGE), slice(EDGE, EXT - EDGE), slice(EXT - EDGE, EXT))
-    for out, cut in zip((low, middle, high), cuts):
-        for i, value in enumerate(add_layers(own, from_prev, from_next, cut)):
-            out[i] = value
+    low, center, high = (add_layers(own, from_prev, from_next, cut) for cut in cuts)
+    for i in range(BZ):
+        s0[i] = by_parity(r, high[i], low[i])
+        s1[i] = by_parity(r, low[i], high[i])
+        middle[i] = center[i]
 
 
 def view_sum(taps):
     return taps[0, MISC, 0] + taps[1, MISC, 0] + taps[2, MISC, 0] + taps[3, MISC, 0]
 
 
-def window_body(taps, ext, low, high, from_prev, from_next, out):
+def window_body(taps, ext, s0, s1, r0, r1, out):
     _, r, _ = position()
     wsum = view_sum(taps)
     for i in range(BZ):
-        total = low[i] + jnp.where(r > 0, from_prev[i], 0.0)
+        total = by_parity(r, s1[i], s0[i]) + jnp.where(r > 0, by_parity(r, r1[i], r0[i]), 0.0)
         out[i, :ROWS] = ext[i, :ROWS] * total / wsum
-        total = high[i] + jnp.where(r < 3, from_next[i], 0.0)
+        total = by_parity(r, s0[i], s1[i]) + jnp.where(r < 3, by_parity(r, r0[i], r1[i]), 0.0)
         out[i, ROWS:] = ext[i, ROWS:] * total / wsum
 
 
-def last_body(taps, ext, middle, from_prev, from_next, out):
+def last_body(taps, ext, middle, r0, r1, out):
     _, r, _ = position()
     wsum = view_sum(taps)
     for i in range(BZ):
-        total = middle[i, :EDGE] + jnp.where(r > 0, from_prev[i], 0.0)
+        total = middle[i, :EDGE] + jnp.where(r > 0, by_parity(r, r1[i], r0[i]), 0.0)
         out[i, :EDGE] = ext[i, EDGE:ROWS] * total / wsum
-        total = middle[i, EDGE:] + jnp.where(r < 3, from_next[i], 0.0)
+        total = middle[i, EDGE:] + jnp.where(r < 3, by_parity(r, r0[i], r1[i]), 0.0)
         out[i, EDGE:] = ext[i, ROWS : EXT - EDGE] * total / wsum
 
 
@@ -520,8 +530,8 @@
                 low, high = call(
                     halves_body, (shape(*QUARTER),) * 2, (c_own, from_prev, from_next), [vmem()] * 3, [], 1_000_000
                 )
-                row_prev = to_row(high, 1)
-                row_next = to_row(low, -1)
+                row_prev = swap_row(low, 0)
+                row_next = swap_row(high, 1)
                 ext = call(
                     window_body,
                     shape(*WINDOW),
@@ -540,8 +550,8 @@
                     [],
                     1_000_000,
                 )
-                row_prev = to_row(high, 1)
-                row_next = to_row(low, -1)
+                row_prev = swap_row(low, 0)
+                row_next = swap_row(high, 1)
                 own = call(
                     last_body,
                     shape(*QUARTER),

time: 149 us -> 147 us (0.987)
  waiting for transfers between devices: 74.5 us -> 68 us
  starting transfers between devices: 46 us -> 49.1 us
    ppermute x2, starting transfers between devices: 10.3 us -> 14.9 us  [collect(): return lax.ppermute(x, AXES, perm)]
    ppermute x4, waiting for transfers between devices: 8.78 us -> 5.12 us  [swap_row(): return lax.ppermute(x, AXES, perm)]
    ppermute x2, waiting for transfers between devices: 20.1 us -> 16.6 us  [collect(): return lax.ppermute(x, AXES, perm)]
where the time goes in v4:
time: 147 us; the launch traced here: 146 us
  waiting for transfers between devices  68 us (46%)
  starting transfers between devices  49.1 us (33%)
  Pallas kernels  25.3 us (17%)
  local copies, waits for them, and re-layouts  2.24 us (2%)
    ppermute x10, waiting for transfers between devices, to_layer(): return lax.ppermute(x, AXES, perm)  26.1 us
    pallas_call x13, Pallas kernels, call(): pl.pallas_call(body, out_shape=outs, in_specs=specs, out_specs=out_specs...  25.3 us
    ppermute x5, starting transfers between devices, spread(): return lax.ppermute(x, AXES, perm)  19.1 us
    ppermute x5, waiting for transfers between devices, spread(): return lax.ppermute(x, AXES, perm)  18.6 us
    ppermute x2, waiting for transfers between devices, collect(): return lax.ppermute(x, AXES, perm)  16.6 us
    ppermute x2, starting transfers between devices, collect(): return lax.ppermute(x, AXES, perm)  14.9 us
    ppermute x10, starting transfers between devices, to_layer(): return lax.ppermute(x, AXES, perm)  8.84 us
    ppermute x4, starting transfers between devices, swap_row(): return lax.ppermute(x, AXES, perm)  6.24 us
  transfers between devices with their start and end apart: 23, of which 15 were waited for; matrix products, arithmetic and copies ran while one was open for 0% of the time, Pallas kernels for 6%

profile of v4, /device:TPU:95, one launch (start us, length us, event | category | flops | bytes accessed | tf_op | source)
XLA Modules:
  0.0 145.5 jit_solution(11567791127125788528)
XLA Ops:
  1.3 4.2 %collective-permute-start.4 = (f32[16,64,128]{2,1,0:T(8,128)S(1)}, f32[16,64,128]{2,1,0:T(8,128)S(1)}, u32[]{:S(2)}, u32[]{:S(2)}) collective-permute-start(f32[16,64,128]{2,1,0:T(8,128)S(1)} %window.1), channel_id=1, source_target_pairs={{0,4},{1,12},{2,0},{3,8},{4,9},{5,1},{6,5},{7,13},{8,29},{9,21},{1... | collective-permute-start | bytes 1572872 | tf_op jit(solution)/shard_map/window/ppermute | solution.py:49
  7.4 2.5 %collective-permute-start = (f32[520,128]{1,0:T(8,128)S(1)}, f32[520,128]{1,0:T(8,128)S(1)}, u32[]{:S(2)}, u32[]{:S(2)}) collective-permute-start(f32[520,128]{1,0:T(8,128)S(1)} %get-tuple-element.28), channel_id=1, source_target_pairs={{0,4},{1,12},{2,0},{3,8},{4,9},{5,1},{6,5},{7,13},{8,29},{9,21},{1... | collective-permute-start | bytes 798728 | tf_op jit(solution)/shard_map/spread/ppermute | solution.py:49
  9.9 2.6 %collective-permute-start.1 = (f32[520,128]{1,0:T(8,128)S(1)}, f32[520,128]{1,0:T(8,128)S(1)}, u32[]{:S(2)}, u32[]{:S(2)}) collective-permute-start(f32[520,128]{1,0:T(8,128)S(1)} %get-tuple-element.29), channel_id=1, source_target_pairs={{0,12},{1,4},{2,8},{3,0},{4,1},{5,9},{6,13},{7,5},{8,21},{9,29},{1... | collective-permute-start | bytes 798728 | tf_op jit(solution)/shard_map/spread/ppermute | solution.py:49
  12.5 7.5 %collective-permute-start.2 = (f32[520,128]{1,0:T(8,128)S(1)}, f32[520,128]{1,0:T(8,128)S(1)}, u32[]{:S(2)}, u32[]{:S(2)}) collective-permute-start(f32[520,128]{1,0:T(8,128)S(1)} %get-tuple-element.30), channel_id=1, source_target_pairs={{0,0},{1,8},{2,4},{3,12},{4,5},{5,13},{6,9},{7,1},{8,25},{9,17},{1... | collective-permute-start | bytes 798728 | tf_op jit(solution)/shard_map/spread/ppermute | solution.py:49
  20.0 2.4 %collective-permute-start.3 = (f32[520,128]{1,0:T(8,128)S(1)}, f32[520,128]{1,0:T(8,128)S(1)}, u32[]{:S(2)}, u32[]{:S(2)}) collective-permute-start(f32[520,128]{1,0:T(8,128)S(1)} %get-tuple-element.31), channel_id=1, source_target_pairs={{0,8},{1,0},{2,12},{3,4},{4,13},{5,5},{6,1},{7,9},{8,17},{9,25},{1... | collective-permute-start | bytes 798728 | tf_op jit(solution)/shard_map/spread/ppermute | solution.py:49
  22.5 10.0 %collective-permute-done.a0 = f32[520,128]{1,0:T(8,128)S(1)} collective-permute-done((f32[520,128]{1,0:T(8,128)S(1)}, f32[520,128]{1,0:T(8,128)S(1)}, u32[]{:S(2)}, u32[]{:S(2)}) %collective-permute-start) | collective-permute-done | bytes 266272 | tf_op jit(solution)/shard_map/spread/ppermute | solution.py:49
  32.5 4.2 %collective-permute-done.2.a2 = f32[520,128]{1,0:T(8,128)S(1)} collective-permute-done((f32[520,128]{1,0:T(8,128)S(1)}, f32[520,128]{1,0:T(8,128)S(1)}, u32[]{:S(2)}, u32[]{:S(2)}) %collective-permute-start.2) | collective-permute-done | bytes 266272 | tf_op jit(solution)/shard_map/spread/ppermute | solution.py:49
  36.7 4.5 %collective-permute-done.3.a3 = f32[520,128]{1,0:T(8,128)S(1)} collective-permute-done((f32[520,128]{1,0:T(8,128)S(1)}, f32[520,128]{1,0:T(8,128)S(1)}, u32[]{:S(2)}, u32[]{:S(2)}) %collective-permute-start.3) | collective-permute-done | bytes 266272 | tf_op jit(solution)/shard_map/spread/ppermute | solution.py:49
  44.6 2.3 %bands.1 = (bf16[128,256]{1,0:T(8,128)(2,1)S(1)}, bf16[128,256]{1,0:T(8,128)(2,1)S(1)}, bf16[4,256,256]{2,1,0:T(8,128)(2,1)S(1)}, bf16[4,256,256]{2,1,0:T(8,128)(2,1)S(1)}) custom-call(f32[4,8,128]{2,1,0:T(8,128)S(1)} %get-tuple-element.32.taps), custom_call_target="tpu_custom_call" | custom-call | flops 30000000 | bytes 16384 | tf_op jit(solution)/shard_map/bands/pallas_call | solution.py:113
  47.3 3.9 %forward.2.fwd = f32[4,16,32,128]{3,2,1,0:T(8,128)S(1)} custom-call(f32[4,8,128]{2,1,0:T(8,128)S(1)} %get-tuple-element.32.taps, f32[16,64,128]{2,1,0:T(8,128)S(1)} %collective-permute-done.5.before, f32[16,64,128]{2,1,0:T(8,128)S(1)} %collective-permute-done.4.own.ext, f32[16,64,128]{2,1,0:T(8,128)S(1)} %collective-permute-done.6.after, ...), custom_call_target="tpu_custom_call" | custom-call | flops 20000000000 | bytes 2179072 | tf_op jit(solution)/shard_map/forward/pallas_call | solution.py:113
  52.2 3.8 %collective-permute-done.7.lower = f32[1536,128]{1,0:T(8,128)S(1)} collective-permute-done((f32[1536,128]{1,0:T(8,128)S(1)}, f32[1536,128]{1,0:T(8,128)S(1)}, u32[]{:S(2)}, u32[]{:S(2)}) %collective-permute-start.7) | collective-permute-done | bytes 786464 | tf_op jit(solution)/shard_map/shift/ppermute | solution.py:63
  56.0 5.1 %back.2 = (f32[15,64,128]{2,1,0:T(8,128)S(1)}, f32[16,64,128]{2,1,0:T(8,128)S(1)}, f32[15,64,128]{2,1,0:T(8,128)S(1)}, f32[4,16,32,128]{3,2,1,0:T(8,128)S(1)}) custom-call(f32[4,8,128]{2,1,0:T(8,128)S(1)} %get-tuple-element.32.taps, f32[4,16,32,128]{3,2,1,0:T(8,128)} %copy-done.6, f32[520,128]{1,0:T(8,128)S(1)} %collective-permute-done.a0, ...), custom_call_target="tpu_custom_call" | custom-call | flops 2000000000 | bytes 4292608 | tf_op jit(solution)/shard_map/back/pallas_call | solution.py:113
  62.7 6.5 %collective-permute-done.9.from_prev = f32[15,64,128]{2,1,0:T(8,128)S(1)} collective-permute-done((f32[15,64,128]{2,1,0:T(8,128)S(1)}, f32[15,64,128]{2,1,0:T(8,128)S(1)}, u32[]{:S(2)}, u32[]{:S(2)}) %collective-permute-start.9) | collective-permute-done | bytes 491552 | tf_op jit(solution)/shard_map/layers_out/ppermute | solution.py:63
  71.2 3.4 %collective-permute-done.11.r0 = f32[16,32,128]{2,1,0:T(8,128)S(1)} collective-permute-done((f32[16,32,128]{2,1,0:T(8,128)S(1)}, f32[16,32,128]{2,1,0:T(8,128)S(1)}, u32[]{:S(2)}, u32[]{:S(2)}) %collective-permute-start.11) | collective-permute-done | bytes 262176 | tf_op jit(solution)/shard_map/rows/ppermute | solution.py:69
  77.3 2.4 %collective-permute-start.13 = (f32[16,64,128]{2,1,0:T(8,128)S(1)}, f32[16,64,128]{2,1,0:T(8,128)S(1)}, u32[]{:S(2)}, u32[]{:S(2)}) collective-permute-start(f32[16,64,128]{2,1,0:T(8,128)S(1)} %rows.5.own.ext), channel_id=1, source_target_pairs={{0,1},{4,5},{8,9},{12,13},{1,17},{5,21},{9,25},{13,29},{17,16},{21... | collective-permute-start | bytes 1572872 | tf_op jit(solution)/shard_map/layers_in/ppermute | solution.py:63
  79.7 3.7 %collective-permute-done.14.after = f32[16,64,128]{2,1,0:T(8,128)S(1)} collective-permute-done((f32[16,64,128]{2,1,0:T(8,128)S(1)}, f32[16,64,128]{2,1,0:T(8,128)S(1)}, u32[]{:S(2)}, u32[]{:S(2)}) %collective-permute-start.14) | collective-permute-done | bytes 524320 | tf_op jit(solution)/shard_map/layers_in/ppermute | solution.py:63
  83.4 5.2 %collective-permute-done.13.before = f32[16,64,128]{2,1,0:T(8,128)S(1)} collective-permute-done((f32[16,64,128]{2,1,0:T(8,128)S(1)}, f32[16,64,128]{2,1,0:T(8,128)S(1)}, u32[]{:S(2)}, u32[]{:S(2)}) %collective-permute-start.13) | collective-permute-done | bytes 524320 | tf_op jit(solution)/shard_map/layers_in/ppermute | solution.py:63
  88.6 3.9 %forward.3.fwd = f32[4,16,32,128]{3,2,1,0:T(8,128)S(1)} custom-call(f32[4,8,128]{2,1,0:T(8,128)S(1)} %get-tuple-element.32.taps, f32[16,64,128]{2,1,0:T(8,128)S(1)} %collective-permute-done.13.before, f32[16,64,128]{2,1,0:T(8,128)S(1)} %rows.5.own.ext, f32[16,64,128]{2,1,0:T(8,128)S(1)} %collective-permute-done.14.after, ...), custom_call_target="tpu_custom_call" | custom-call | flops 2000000000 | bytes 2179072 | tf_op jit(solution)/shard_map/forward/pallas_call | solution.py:113
  92.5 3.8 %back.3 = (f32[15,64,128]{2,1,0:T(8,128)S(1)}, f32[16,64,128]{2,1,0:T(8,128)S(1)}, f32[15,64,128]{2,1,0:T(8,128)S(1)}) custom-call(f32[4,8,128]{2,1,0:T(8,128)S(1)} %get-tuple-element.32.taps, f32[4,16,32,128]{3,2,1,0:T(8,128)S(1)} %forward.3.fwd, f32[4,16,32,128]{3,2,1,0:T(8,128)S(1)} %get-tuple-element.44.rec, ...), custom_call_target="tpu_custom_call" | custom-call | flops 2000000000 | bytes 2703360 | tf_op jit(solution)/shard_map/back/pallas_call | solution.py:113
  97.9 6.5 %collective-permute-done.15.from_prev = f32[15,64,128]{2,1,0:T(8,128)S(1)} collective-permute-done((f32[15,64,128]{2,1,0:T(8,128)S(1)}, f32[15,64,128]{2,1,0:T(8,128)S(1)}, u32[]{:S(2)}, u32[]{:S(2)}) %collective-permute-start.15) | collective-permute-done | bytes 491552 | tf_op jit(solution)/shard_map/layers_out/ppermute | solution.py:63
  104.5 3.7 %collective-permute-start.17 = (f32[16,16,128]{2,1,0:T(8,128)S(1)}, f32[16,16,128]{2,1,0:T(8,128)S(1)}, u32[]{:S(2)}, u32[]{:S(2)}) collective-permute-start(f32[16,16,128]{2,1,0:T(8,128)S(1)} %get-tuple-element.49), channel_id=1, source_target_pairs={{0,4},{4,0},{8,12},{12,8},{1,5},{5,1},{9,13},{13,9},{17,21},{21,17... | collective-permute-start | bytes 393224 | tf_op jit(solution)/shard_map/rows/ppermute | solution.py:69
  111.4 13.0 %collective-permute-start.21 = (f32[16,32,128]{2,1,0:T(8,128)S(1)}, f32[16,32,128]{2,1,0:T(8,128)S(1)}, u32[]{:S(2)}, u32[]{:S(2)}) collective-permute-start(f32[16,32,128]{2,1,0:T(8,128)S(1)} %rows.7), channel_id=1, source_target_pairs={{0,0},{8,1},{4,2},{12,3},{5,4},{13,5},{9,6},{1,7},{25,8},{17,9},{2... | collective-permute-start | bytes 786440 | tf_op jit(solution)/shard_map/result/ppermute | solution.py:54
  124.4 1.9 %collective-permute-start.19 = (f32[16,32,128]{2,1,0:T(8,128)S(1)}, f32[16,32,128]{2,1,0:T(8,128)S(1)}, u32[]{:S(2)}, u32[]{:S(2)}) collective-permute-start(f32[16,32,128]{2,1,0:T(8,128)S(1)} %rows.7), channel_id=1, source_target_pairs={{4,0},{12,1},{0,2},{8,3},{9,4},{1,5},{5,6},{13,7},{29,8},{21,9},{2... | collective-permute-start | bytes 786440 | tf_op jit(solution)/shard_map/result/ppermute | solution.py:54
  126.3 15.7 %collective-permute-done.21.c2 = f32[16,32,128]{2,1,0:T(8,128)S(1)} collective-permute-done((f32[16,32,128]{2,1,0:T(8,128)S(1)}, f32[16,32,128]{2,1,0:T(8,128)S(1)}, u32[]{:S(2)}, u32[]{:S(2)}) %collective-permute-start.21) | collective-permute-done | bytes 262176 | tf_op jit(solution)/shard_map/result/ppermute | solution.py:54
  (49 shorter events, 22.0 us)
Async XLA Ops:
  1.2 4.9 %copy-start.5 = (f32[1,31]{1,0:T(1,128)S(1)}, f32[1,31]{1,0:T(1,128)}, u32[]{:S(2)}) copy-start(f32[1,31]{1,0:T(1,128)} %psf_x.1) | copy-start | bytes 376
  1.3 21.1 %collective-permute-start.4 = (f32[16,64,128]{2,1,0:T(8,128)S(1)}, f32[16,64,128]{2,1,0:T(8,128)S(1)}, u32[]{:S(2)}, u32[]{:S(2)}) collective-permute-start(f32[16,64,128]{2,1,0:T(8,128)S(1)} %window.1), channel_id=1, source_target_pairs={{0,4},{1,12},{2,0},{3,8},{4,9},{5,1},{6,5},{7,13},{8,29},{9,21},{1... | collective-permute-start | bytes 1572872 | tf_op jit(solution)/shard_map/window/ppermute | solution.py:49
  7.4 25.0 %collective-permute-start = (f32[520,128]{1,0:T(8,128)S(1)}, f32[520,128]{1,0:T(8,128)S(1)}, u32[]{:S(2)}, u32[]{:S(2)}) collective-permute-start(f32[520,128]{1,0:T(8,128)S(1)} %get-tuple-element.28), channel_id=1, source_target_pairs={{0,4},{1,12},{2,0},{3,8},{4,9},{5,1},{6,5},{7,13},{8,29},{9,21},{1... | collective-permute-start | bytes 798728 | tf_op jit(solution)/shard_map/spread/ppermute | solution.py:49
  9.9 22.6 %collective-permute-start.1 = (f32[520,128]{1,0:T(8,128)S(1)}, f32[520,128]{1,0:T(8,128)S(1)}, u32[]{:S(2)}, u32[]{:S(2)}) collective-permute-start(f32[520,128]{1,0:T(8,128)S(1)} %get-tuple-element.29), channel_id=1, source_target_pairs={{0,12},{1,4},{2,8},{3,0},{4,1},{5,9},{6,13},{7,5},{8,21},{9,29},{1... | collective-permute-start | bytes 798728 | tf_op jit(solution)/shard_map/spread/ppermute | solution.py:49
  12.5 24.2 %collective-permute-start.2 = (f32[520,128]{1,0:T(8,128)S(1)}, f32[520,128]{1,0:T(8,128)S(1)}, u32[]{:S(2)}, u32[]{:S(2)}) collective-permute-start(f32[520,128]{1,0:T(8,128)S(1)} %get-tuple-element.30), channel_id=1, source_target_pairs={{0,0},{1,8},{2,4},{3,12},{4,5},{5,13},{6,9},{7,1},{8,25},{9,17},{1... | collective-permute-start | bytes 798728 | tf_op jit(solution)/shard_map/spread/ppermute | solution.py:49
  20.0 21.1 %collective-permute-start.3 = (f32[520,128]{1,0:T(8,128)S(1)}, f32[520,128]{1,0:T(8,128)S(1)}, u32[]{:S(2)}, u32[]{:S(2)}) collective-permute-start(f32[520,128]{1,0:T(8,128)S(1)} %get-tuple-element.31), channel_id=1, source_target_pairs={{0,8},{1,0},{2,12},{3,4},{4,13},{5,5},{6,1},{7,9},{8,17},{9,25},{1... | collective-permute-start | bytes 798728 | tf_op jit(solution)/shard_map/spread/ppermute | solution.py:49
  22.4 24.5 %collective-permute-start.6 = (f32[16,64,128]{2,1,0:T(8,128)S(1)}, f32[16,64,128]{2,1,0:T(8,128)S(1)}, u32[]{:S(2)}, u32[]{:S(2)}) collective-permute-start(f32[16,64,128]{2,1,0:T(8,128)S(1)} %collective-permute-done.4.own.ext), channel_id=1, source_target_pairs={{0,194},{4,198},{8,202},{12,206},{1,0},{5,4},{9,8},{13,12},{17,1},... | collective-permute-start | bytes 1572872 | tf_op jit(solution)/shard_map/layers_in/ppermute | solution.py:63
  32.5 14.8 %collective-permute-start.5 = (f32[16,64,128]{2,1,0:T(8,128)S(1)}, f32[16,64,128]{2,1,0:T(8,128)S(1)}, u32[]{:S(2)}, u32[]{:S(2)}) collective-permute-start(f32[16,64,128]{2,1,0:T(8,128)S(1)} %collective-permute-done.4.own.ext), channel_id=1, source_target_pairs={{0,1},{4,5},{8,9},{12,13},{1,17},{5,21},{9,25},{13,29},{17,16},{21... | collective-permute-start | bytes 1572872 | tf_op jit(solution)/shard_map/layers_in/ppermute | solution.py:63
  43.1 13.0 %collective-permute-start.7 = (f32[1536,128]{1,0:T(8,128)S(1)}, f32[1536,128]{1,0:T(8,128)S(1)}, u32[]{:S(2)}, u32[]{:S(2)}) collective-permute-start(f32[1536,128]{1,0:T(8,128)S(1)} %get-tuple-element.35), channel_id=1, source_target_pairs={{0,1},{4,5},{8,9},{12,13},{1,17},{5,21},{9,25},{13,29},{17,16},{21... | collective-permute-start | bytes 2359304 | tf_op jit(solution)/shard_map/shift/ppermute | solution.py:63
  44.4 11.7 %collective-permute-start.8 = (f32[1536,128]{1,0:T(8,128)S(1)}, f32[1536,128]{1,0:T(8,128)S(1)}, u32[]{:S(2)}, u32[]{:S(2)}) collective-permute-start(f32[1536,128]{1,0:T(8,128)S(1)} %get-tuple-element.36), channel_id=1, source_target_pairs={{0,194},{4,198},{8,202},{12,206},{1,0},{5,4},{9,8},{13,12},{17,1},... | collective-permute-start | bytes 2359304 | tf_op jit(solution)/shard_map/shift/ppermute | solution.py:63
  61.2 8.1 %collective-permute-start.9 = (f32[15,64,128]{2,1,0:T(8,128)S(1)}, f32[15,64,128]{2,1,0:T(8,128)S(1)}, u32[]{:S(2)}, u32[]{:S(2)}) collective-permute-start(f32[15,64,128]{2,1,0:T(8,128)S(1)} %get-tuple-element.40), channel_id=1, source_target_pairs={{0,1},{4,5},{8,9},{12,13},{1,17},{5,21},{9,25},{13,29},{17,16},{21... | collective-permute-start | bytes 1474568 | tf_op jit(solution)/shard_map/layers_out/ppermute | solution.py:63
  62.5 6.7 %collective-permute-start.10 = (f32[15,64,128]{2,1,0:T(8,128)S(1)}, f32[15,64,128]{2,1,0:T(8,128)S(1)}, u32[]{:S(2)}, u32[]{:S(2)}) collective-permute-start(f32[15,64,128]{2,1,0:T(8,128)S(1)} %get-tuple-element.41), channel_id=1, source_target_pairs={{0,194},{4,198},{8,202},{12,206},{1,0},{5,4},{9,8},{13,12},{17,1},... | collective-permute-start | bytes 1474568 | tf_op jit(solution)/shard_map/layers_out/ppermute | solution.py:63
  69.4 5.3 %collective-permute-start.11 = (f32[16,32,128]{2,1,0:T(8,128)S(1)}, f32[16,32,128]{2,1,0:T(8,128)S(1)}, u32[]{:S(2)}, u32[]{:S(2)}) collective-permute-start(f32[16,32,128]{2,1,0:T(8,128)S(1)} %get-tuple-element.42.s0), channel_id=1, source_target_pairs={{0,4},{4,0},{8,12},{12,8},{1,5},{5,1},{9,13},{13,9},{17,21},{21,17... | collective-permute-start | bytes 786440 | tf_op jit(solution)/shard_map/rows/ppermute | solution.py:69
  70.6 4.1 %collective-permute-start.12 = (f32[16,32,128]{2,1,0:T(8,128)S(1)}, f32[16,32,128]{2,1,0:T(8,128)S(1)}, u32[]{:S(2)}, u32[]{:S(2)}) collective-permute-start(f32[16,32,128]{2,1,0:T(8,128)S(1)} %get-tuple-element.43.s1), channel_id=1, source_target_pairs={{0,0},{4,8},{8,4},{12,12},{1,1},{5,9},{9,5},{13,13},{17,17},{21,25... | collective-permute-start | bytes 786440 | tf_op jit(solution)/shard_map/rows/ppermute | solution.py:69
  75.6 7.8 %collective-permute-start.14 = (f32[16,64,128]{2,1,0:T(8,128)S(1)}, f32[16,64,128]{2,1,0:T(8,128)S(1)}, u32[]{:S(2)}, u32[]{:S(2)}) collective-permute-start(f32[16,64,128]{2,1,0:T(8,128)S(1)} %rows.5.own.ext), channel_id=1, source_target_pairs={{0,194},{4,198},{8,202},{12,206},{1,0},{5,4},{9,8},{13,12},{17,1},... | collective-permute-start | bytes 1572872 | tf_op jit(solution)/shard_map/layers_in/ppermute | solution.py:63
  77.3 11.3 %collective-permute-start.13 = (f32[16,64,128]{2,1,0:T(8,128)S(1)}, f32[16,64,128]{2,1,0:T(8,128)S(1)}, u32[]{:S(2)}, u32[]{:S(2)}) collective-permute-start(f32[16,64,128]{2,1,0:T(8,128)S(1)} %rows.5.own.ext), channel_id=1, source_target_pairs={{0,1},{4,5},{8,9},{12,13},{1,17},{5,21},{9,25},{13,29},{17,16},{21... | collective-permute-start | bytes 1572872 | tf_op jit(solution)/shard_map/layers_in/ppermute | solution.py:63
  96.3 8.1 %collective-permute-start.15 = (f32[15,64,128]{2,1,0:T(8,128)S(1)}, f32[15,64,128]{2,1,0:T(8,128)S(1)}, u32[]{:S(2)}, u32[]{:S(2)}) collective-permute-start(f32[15,64,128]{2,1,0:T(8,128)S(1)} %get-tuple-element.46), channel_id=1, source_target_pairs={{0,1},{4,5},{8,9},{12,13},{1,17},{5,21},{9,25},{13,29},{17,16},{21... | collective-permute-start | bytes 1474568 | tf_op jit(solution)/shard_map/layers_out/ppermute | solution.py:63
  96.4 8.0 %collective-permute-start.16 = (f32[15,64,128]{2,1,0:T(8,128)S(1)}, f32[15,64,128]{2,1,0:T(8,128)S(1)}, u32[]{:S(2)}, u32[]{:S(2)}) collective-permute-start(f32[15,64,128]{2,1,0:T(8,128)S(1)} %get-tuple-element.47), channel_id=1, source_target_pairs={{0,194},{4,198},{8,202},{12,206},{1,0},{5,4},{9,8},{13,12},{17,1},... | collective-permute-start | bytes 1474568 | tf_op jit(solution)/shard_map/layers_out/ppermute | solution.py:63
  104.5 6.1 %collective-permute-start.17 = (f32[16,16,128]{2,1,0:T(8,128)S(1)}, f32[16,16,128]{2,1,0:T(8,128)S(1)}, u32[]{:S(2)}, u32[]{:S(2)}) collective-permute-start(f32[16,16,128]{2,1,0:T(8,128)S(1)} %get-tuple-element.49), channel_id=1, source_target_pairs={{0,4},{4,0},{8,12},{12,8},{1,5},{5,1},{9,13},{13,9},{17,21},{21,17... | collective-permute-start | bytes 393224 | tf_op jit(solution)/shard_map/rows/ppermute | solution.py:69
  108.2 2.4 %collective-permute-start.18 = (f32[16,16,128]{2,1,0:T(8,128)S(1)}, f32[16,16,128]{2,1,0:T(8,128)S(1)}, u32[]{:S(2)}, u32[]{:S(2)}) collective-permute-start(f32[16,16,128]{2,1,0:T(8,128)S(1)} %get-tuple-element.50), channel_id=1, source_target_pairs={{0,0},{4,8},{8,4},{12,12},{1,1},{5,9},{9,5},{13,13},{17,17},{21,25... | collective-permute-start | bytes 393224 | tf_op jit(solution)/shard_map/rows/ppermute | solution.py:69
  111.4 30.6 %collective-permute-start.21 = (f32[16,32,128]{2,1,0:T(8,128)S(1)}, f32[16,32,128]{2,1,0:T(8,128)S(1)}, u32[]{:S(2)}, u32[]{:S(2)}) collective-permute-start(f32[16,32,128]{2,1,0:T(8,128)S(1)} %rows.7), channel_id=1, source_target_pairs={{0,0},{8,1},{4,2},{12,3},{5,4},{13,5},{9,6},{1,7},{25,8},{17,9},{2... | collective-permute-start | bytes 786440 | tf_op jit(solution)/shard_map/result/ppermute | solution.py:54
  124.4 18.5 %collective-permute-start.19 = (f32[16,32,128]{2,1,0:T(8,128)S(1)}, f32[16,32,128]{2,1,0:T(8,128)S(1)}, u32[]{:S(2)}, u32[]{:S(2)}) collective-permute-start(f32[16,32,128]{2,1,0:T(8,128)S(1)} %rows.7), channel_id=1, source_target_pairs={{4,0},{12,1},{0,2},{8,3},{9,4},{1,5},{5,6},{13,7},{29,8},{21,9},{2... | collective-permute-start | bytes 786440 | tf_op jit(solution)/shard_map/result/ppermute | solution.py:54
  142.1 1.5 %collective-permute-start.22 = (f32[16,32,128]{2,1,0:T(8,128)S(1)}, f32[16,32,128]{2,1,0:T(8,128)S(1)}, u32[]{:S(2)}, u32[]{:S(2)}) collective-permute-start(f32[16,32,128]{2,1,0:T(8,128)S(1)} %collective-permute-done.21.c2), channel_id=1, source_target_pairs={{0,1},{1,0},{2,3},{3,2},{4,5},{5,4},{6,7},{7,6},{8,9},{9,8},{10,11... | collective-permute-start | bytes 786440 | tf_op jit(solution)/shard_map/result/ppermute | solution.py:58
  142.9 1.5 %collective-permute-start.20 = (f32[16,32,128]{2,1,0:T(8,128)S(1)}, f32[16,32,128]{2,1,0:T(8,128)S(1)}, u32[]{:S(2)}, u32[]{:S(2)}) collective-permute-start(f32[16,32,128]{2,1,0:T(8,128)S(1)} %collective-permute-done.19.c0), channel_id=1, source_target_pairs={{0,1},{1,0},{2,3},{3,2},{4,5},{5,4},{6,7},{7,6},{8,9},{9,8},{10,11... | collective-permute-start | bytes 786440 | tf_op jit(solution)/shard_map/result/ppermute | solution.py:58
  (6 other events, 21.7 us)
